TPU v7x, 32 devices: a whole 2x2x4 slice. The times are simulated.
32 devices in a mesh: ctx: 16 (over z, y, core), head: 2 (over x).
Axes of the slice: x: 2, y: 2, z: 4, core: 2. Of those that a mesh axis runs over, the one named last changes fastest.
Arguments:
- latent_raw: bfloat16 [2048, 576], P(('ctx', 'head')), may hold values from -6 to 6
- kv_gain: float32 [512], replicated, may hold values from 0.1 to 1.9
- query_nope: bfloat16 [2048, 8192], P('ctx', 'head'), may hold values from -144 to 144
- query_rope: bfloat16 [2048, 4096], P('ctx', 'head'), may hold values from -6 to 6
- key_up: bfloat16 [64, 128, 512], P('head'), may hold values from -0.5 to 0.5
- value_up: bfloat16 [64, 512, 128], P('head'), may hold values from -0.25 to 0.25
- doc_lengths: int32 [4], replicated, may hold values from 1 to 896, 2048 in all
Outputs:
- attended: bfloat16 [2048, 8192], P('ctx', 'head')
Inputs may be any that keep to these rules, and one draw needn't show every extreme that they name: `doc_lengths`: documents lie end to end over all 2048 positions; the longest has exactly 896 positions.
All inputs are finite; a program needn't handle non-finite values.
Results may differ from a plain program's by a relative error of at most 0.012.
The roundings to bfloat16 on the way count: a program that leaves them out, or rounds other values in their place, can miss the bound.
Values may be sent and summed in bfloat16 or wider, within the bound.
No kernel may reach another device: no remote copies, remote signals or barrier semaphores. Data moves between devices by JAX's collectives and lax.ppermute only.
A program may use at most 64 MiB of HBM per device.

v0:
```python
import jax
import jax.numpy as jnp
from jax import lax
from jax.sharding import PartitionSpec as P

HOPS = 7


epsilon = 1e-06
masked_score = -1e30


def shifted(value, axis, steps):
    count = lax.axis_size(axis)
    leading, last = (max(0, -steps), min(count, count - steps))
    return lax.ppermute(value, axis, [(source, source + steps) for source in range(leading, last)])


def doc_begin(positions, starts):
    inside = starts[None, :] <= positions[:, None]
    return jnp.max(jnp.where(inside, starts[None, :], 0), axis=1)


def rotation(offsets, rope_half):
    frequency = 10000.0 ** (-2.0 * jnp.arange(rope_half, dtype=jnp.float32) / (2 * rope_half))
    angles = offsets.astype(jnp.float32)[:, None] * frequency[None, :]
    return (jnp.cos(angles), jnp.sin(angles))


def rotate(values, cos_table, sin_table):
    rope_half = cos_table.shape[-1]
    first_half = values[..., :rope_half]
    second_half = values[..., rope_half:]
    return jnp.concatenate(
        [
            first_half * cos_table - second_half * sin_table,
            second_half * cos_table + first_half * sin_table,
        ],
        axis=-1,
    )


def shards(latent_raw, kv_gain, query_nope, query_rope, key_up, value_up, doc_lengths):
    row_count = query_nope.shape[0]
    head_count = key_up.shape[0]
    nope_width = key_up.shape[1]
    latent_width = key_up.shape[2]
    value_width = value_up.shape[2]
    full_width = latent_raw.shape[1]
    rope_width = full_width - latent_width
    rope_half = rope_width // 2
    half_rows = latent_raw.shape[0]
    score_scale = (nope_width + rope_width) ** (-0.5)
    ctx_index = lax.axis_index("ctx")
    head_index = lax.axis_index("head")
    starts = jnp.cumsum(doc_lengths) - doc_lengths
    own_pos = (
        ctx_index * row_count + head_index * half_rows + jnp.arange(half_rows, dtype=jnp.int32)
    )
    own_begin = doc_begin(own_pos, starts)
    cos_own, sin_own = rotation(own_pos - own_begin, rope_half)
    raw_rows = latent_raw.astype(jnp.float32)
    latent_part = raw_rows[:, :latent_width]
    normed = (
        latent_part
        * lax.rsqrt(jnp.mean(latent_part * latent_part, axis=1, keepdims=True) + epsilon)
        * kv_gain
    )
    kv_half = jnp.concatenate(
        [normed, rotate(raw_rows[:, latent_width:], cos_own, sin_own)], axis=1
    ).astype(jnp.bfloat16)
    flat_rows = lax.all_gather(kv_half.reshape(-1, 128), "head", axis=0, tiled=True)
    query_pos = ctx_index * row_count + jnp.arange(row_count, dtype=jnp.int32)
    query_begin = doc_begin(query_pos, starts)
    cos_query, sin_query = rotation(query_pos - query_begin, rope_half)
    absorbed = jnp.einsum(
        "thn,hnr->thr",
        query_nope.reshape(row_count, head_count, nope_width),
        key_up,
        preferred_element_type=jnp.float32,
    ).astype(jnp.bfloat16)
    rope_rows = query_rope.reshape(row_count, head_count, rope_width).astype(jnp.float32)
    rotated = rotate(rope_rows, cos_query[:, None, :], sin_query[:, None, :]).astype(jnp.bfloat16)
    queries = jnp.concatenate([absorbed, rotated], axis=2)

    def live_mask(first_pos):
        key_pos = first_pos + jnp.arange(row_count, dtype=jnp.int32)
        key_begin = doc_begin(key_pos, starts)
        return (
            (key_pos[None, :] <= query_pos[:, None])
            & (key_begin[None, :] == query_begin[:, None])
            & (key_pos[None, :] >= 0)
        )

    def attend(carry_state, key_flat, live_pairs):
        running_max, running_total, running_sum = carry_state
        key_block = key_flat.reshape(row_count, full_width)
        scores = (
            jnp.einsum("thc,sc->hts", queries, key_block, preferred_element_type=jnp.float32)
            * score_scale
        )
        scores = jnp.where(live_pairs[None], scores, masked_score)
        new_max = jnp.maximum(running_max, jnp.max(scores, axis=2))
        factor = jnp.exp(running_max - new_max)
        weights = jnp.where(live_pairs[None], jnp.exp(scores - new_max[:, :, None]), 0.0)
        new_total = running_total * factor + jnp.sum(weights, axis=2)
        new_sum = running_sum * factor[:, :, None] + jnp.einsum(
            "hts,sr->htr",
            weights.astype(jnp.bfloat16),
            key_block[:, :latent_width],
            preferred_element_type=jnp.float32,
        )
        return (new_max, new_total, new_sum)

    def visit_block(carry_state, key_flat, first_pos):
        live_pairs = live_mask(first_pos)
        return attend(carry_state, key_flat, live_pairs)

    start_state = (
        jnp.full((head_count, row_count), masked_score, jnp.float32),
        jnp.zeros((head_count, row_count), jnp.float32),
        jnp.zeros((head_count, row_count, latent_width), jnp.float32),
    )
    carry_state = visit_block(start_state, flat_rows, ctx_index * row_count)

    def hop_step(step_index, loop_carry):
        loop_state, moving = loop_carry
        moving = shifted(moving, "ctx", 1)
        loop_state = visit_block(loop_state, moving, (ctx_index - 1 - step_index) * row_count)
        return (loop_state, moving)

    carry_state, unused = lax.fori_loop(0, HOPS, hop_step, (carry_state, flat_rows))
    running_max, running_total, running_sum = carry_state
    mixed_latent = (running_sum / running_total[:, :, None]).astype(jnp.bfloat16)
    attended = jnp.einsum(
        "htr,hrv->thv", mixed_latent, value_up, preferred_element_type=jnp.float32
    )
    return attended.astype(jnp.bfloat16).reshape(row_count, head_count * value_width)


def solution(mesh):
    return jax.shard_map(
        shards,
        mesh=mesh,
        in_specs=(
            P(("ctx", "head"), None),
            P(),
            P("ctx", "head"),
            P("ctx", "head"),
            P("head", None, None),
            P("head", None, None),
            P(),
        ),
        out_specs=P("ctx", "head"),
        check_vma=False,
    )
```

profile of v0, /device:TPU:24, one launch (start us, length us, event | category | flops | bytes accessed | tf_op | source)
XLA Modules:
  0.0 158.6 jit_solution(8299188779577973958)
XLA Ops:
  0.0 0.9 reduce-window.9
  0.9 0.7 bitcast_subtract_fusion
  1.7 1.0 copy.47
  3.0 0.8 multiply_convert_fusion
  4.2 5.0 %all_gather.3 = bf16[576,128]{1,0:T(8,128)(2,1)S(1)} all-gather(bf16[288,128]{1,0:T(8,128)(2,1)S(1)} %convert_element_type.58), channel_id=1, replica_groups=mesh['ctx'=16,'head'=2] {'head'}, dimensions={0}, use_global_device_ids=true | all-gather | bytes 221184 | tf_op jit(solution)/shard_map/all_gather | solution.py:72
  9.6 1.2 copy.51
  11.2 3.5 %convert_bitcast_fusion = bf16[128,32,512]{0,2,1:T(8,128)(2,1)S(1)} fusion(bf16[32,128,512]{2,1,0:T(8,128)(2,1)} %param.13, bf16[128,4096]{1,0:T(8,128)(2,1)S(1)} %copy-done), kind=kOutput, calls=%fused_computation.28 | convolution fusion | flops 538968064 | bytes 9437184 | tf_op jit(solution)/shard_map/thn,hnr->thr/dot_general | solution.py:76
  14.7 1.0 fusion.17
  16.3 4.0 %broadcast_add_fusion = f32[32,128,512]{2,1,0:T(8,128)} fusion(f32[32,128]{1,0:T(8,128)S(1)} %get-tuple-element.295, f32[128,128,32]{1,0,2:T(8,128)S(1)} %get-tuple-element.300, f32[32,128]{1,0:T(8,128)S(1)} %broadcast_maximum_fusion, pred[128,128]{0,1:T(8,128)(4,1)S(1)} %and_and_fusion.1, bf16[128,576]{1,0:T(8,128)(2,1)S(1)} %reshape.310), kind=kOutput, calls=%fused_computation.27 | convolution fusion | flops 541589504 | bytes 10665984 | tf_op jit(solution)/shard_map/hts,sr->htr/dot_general | solution.py:107
  20.4 2.3 %pad_maximum_fusion = bf16[128,32,576]{0,2,1:T(8,128)(2,1)} fusion(bf16[128,32,32]{0,2,1:T(8,128)(2,1)S(1)} %get-tuple-element.292, bf16[128,32,32]{0,2,1:T(8,128)(2,1)S(1)} %get-tuple-element.291, bf16[128,32,512]{0,2,1:T(8,128)(2,1)S(1)} %convert_bitcast_fusion), kind=kLoop, calls=%fused_computation.26 | loop fusion | flops 14155776 | bytes 9437184 | tf_op jit(solution)/shard_map/concatenate | solution.py:84
  22.7 128.0 %while.22 = (s32[]{:T(128)}, f32[32,128]{1,0:T(8,128)S(1)}, f32[32,128]{1,0:T(8,128)S(1)}, f32[32,128,512]{2,1,0:T(8,128)}, bf16[576,128]{1,0:T(8,128)(2,1)S(1)}...) while((s32[]{:T(128)}, f32[32,128]{1,0:T(8,128)S(1)}, ...), condition=%wide.region_10.11_spmd.clone, body=%wide.region_6.10_spmd.clone.sunk | while | flops 1151936384 | bytes 96686600 | solution.py:132
  22.7 1.9 %collective-permute-start = (bf16[576,128]{1,0:T(8,128)(2,1)S(1)}, bf16[576,128]{1,0:T(8,128)(2,1)S(1)}, u32[]{:S(2)}, u32[]{:S(2)}) collective-permute-start(bf16[576,128]{1,0:T(8,128)(2,1)S(1)} %get-tuple-element.390), channel_id=1, source_target_pairs={{0,2},{2,4},{4,6},{6,8},{8,10},{10,12},{12,14},{14,16},{16,18},{18... | collective-permute-start | bytes 442376 | tf_op jit(solution)/shard_map/while/body/eval_jaxpr/ppermute | solution.py:16
  24.9 5.2 %collective-permute-done = bf16[576,128]{1,0:T(8,128)(2,1)S(1)} collective-permute-done((bf16[576,128]{1,0:T(8,128)(2,1)S(1)}, bf16[576,128]{1,0:T(8,128)(2,1)S(1)}, u32[]{:S(2)}, u32[]{:S(2)}) %collective-permute-start) | collective-permute-done | bytes 147488 | tf_op jit(solution)/shard_map/while/body/eval_jaxpr/ppermute | solution.py:16
  30.2 3.6 %fusion.53 = (f32[32,128]{1,0:T(8,128)S(1)}, f32[128,128,32]{1,0,2:T(8,128)S(1)}) fusion(pred[128,128]{0,1:T(8,128)(4,1)S(1)} %and_and_fusion.3, bf16[128,32,576]{0,2,1:T(8,128)(2,1)} %get-tuple-element.406, bf16[128,576]{1,0:T(8,128)(2,1)S(1)} %reshape.320), kind=kOutput, calls=%fused_computation.4.clone.1 | convolution fusion | flops 605548544 | bytes 6995968 | tf_op jit(solution)/shard_map/while/body/eval_jaxpr/thc,sc->hts/dot_general | solution.py:99
  35.0 2.7 %multiply_add_fusion.5 = f32[32,128,512]{2,1,0:T(8,128)S(1)} fusion(f32[32,128,512]{2,1,0:T(8,128)S(1)} %copy-done.1, f32[32,128]{1,0:T(8,128)S(1)} %get-tuple-element.373, f32[128,128,32]{1,0,2:T(8,128)S(1)} %get-tuple-element.371, f32[32,128]{1,0:T(8,128)S(1)} %max.11, pred[128,128]{0,1:T(8,128)(4,1)S(1)} %and_and_fusion.3, ...), kind=kOutput, calls=%fused_computation.1.clone.1 | convolution fusion | flops 543686656 | bytes 19054592 | tf_op jit(solution)/shard_map/while/body/eval_jaxpr/hts,sr->htr/dot_general | solution.py:107
  37.8 3.2 %copy-done.2 = f32[32,128,512]{2,1,0:T(8,128)} copy-done((f32[32,128,512]{2,1,0:T(8,128)}, f32[32,128,512]{2,1,0:T(8,128)S(1)}, u32[]{:S(2)}) %copy-start.2) | copy-done | bytes 8388632 | tf_op jit(solution)/shard_map/while
  41.0 1.9 %collective-permute-start = (bf16[576,128]{1,0:T(8,128)(2,1)S(1)}, bf16[576,128]{1,0:T(8,128)(2,1)S(1)}, u32[]{:S(2)}, u32[]{:S(2)}) collective-permute-start(bf16[576,128]{1,0:T(8,128)(2,1)S(1)} %get-tuple-element.390), channel_id=1, source_target_pairs={{0,2},{2,4},{4,6},{6,8},{8,10},{10,12},{12,14},{14,16},{16,18},{18... | collective-permute-start | bytes 442376 | tf_op jit(solution)/shard_map/while/body/eval_jaxpr/ppermute | solution.py:16
  43.1 5.2 %collective-permute-done = bf16[576,128]{1,0:T(8,128)(2,1)S(1)} collective-permute-done((bf16[576,128]{1,0:T(8,128)(2,1)S(1)}, bf16[576,128]{1,0:T(8,128)(2,1)S(1)}, u32[]{:S(2)}, u32[]{:S(2)}) %collective-permute-start) | collective-permute-done | bytes 147488 | tf_op jit(solution)/shard_map/while/body/eval_jaxpr/ppermute | solution.py:16
  48.5 3.6 %fusion.53 = (f32[32,128]{1,0:T(8,128)S(1)}, f32[128,128,32]{1,0,2:T(8,128)S(1)}) fusion(pred[128,128]{0,1:T(8,128)(4,1)S(1)} %and_and_fusion.3, bf16[128,32,576]{0,2,1:T(8,128)(2,1)} %get-tuple-element.406, bf16[128,576]{1,0:T(8,128)(2,1)S(1)} %reshape.320), kind=kOutput, calls=%fused_computation.4.clone.1 | convolution fusion | flops 605548544 | bytes 6995968 | tf_op jit(solution)/shard_map/while/body/eval_jaxpr/thc,sc->hts/dot_general | solution.py:99
  53.3 2.7 %multiply_add_fusion.5 = f32[32,128,512]{2,1,0:T(8,128)S(1)} fusion(f32[32,128,512]{2,1,0:T(8,128)S(1)} %copy-done.1, f32[32,128]{1,0:T(8,128)S(1)} %get-tuple-element.373, f32[128,128,32]{1,0,2:T(8,128)S(1)} %get-tuple-element.371, f32[32,128]{1,0:T(8,128)S(1)} %max.11, pred[128,128]{0,1:T(8,128)(4,1)S(1)} %and_and_fusion.3, ...), kind=kOutput, calls=%fused_computation.1.clone.1 | convolution fusion | flops 543686656 | bytes 19054592 | tf_op jit(solution)/shard_map/while/body/eval_jaxpr/hts,sr->htr/dot_general | solution.py:107
  56.1 3.2 %copy-done.2 = f32[32,128,512]{2,1,0:T(8,128)} copy-done((f32[32,128,512]{2,1,0:T(8,128)}, f32[32,128,512]{2,1,0:T(8,128)S(1)}, u32[]{:S(2)}) %copy-start.2) | copy-done | bytes 8388632 | tf_op jit(solution)/shard_map/while
  59.3 1.9 %collective-permute-start = (bf16[576,128]{1,0:T(8,128)(2,1)S(1)}, bf16[576,128]{1,0:T(8,128)(2,1)S(1)}, u32[]{:S(2)}, u32[]{:S(2)}) collective-permute-start(bf16[576,128]{1,0:T(8,128)(2,1)S(1)} %get-tuple-element.390), channel_id=1, source_target_pairs={{0,2},{2,4},{4,6},{6,8},{8,10},{10,12},{12,14},{14,16},{16,18},{18... | collective-permute-start | bytes 442376 | tf_op jit(solution)/shard_map/while/body/eval_jaxpr/ppermute | solution.py:16
  61.4 5.2 %collective-permute-done = bf16[576,128]{1,0:T(8,128)(2,1)S(1)} collective-permute-done((bf16[576,128]{1,0:T(8,128)(2,1)S(1)}, bf16[576,128]{1,0:T(8,128)(2,1)S(1)}, u32[]{:S(2)}, u32[]{:S(2)}) %collective-permute-start) | collective-permute-done | bytes 147488 | tf_op jit(solution)/shard_map/while/body/eval_jaxpr/ppermute | solution.py:16
  66.8 3.6 %fusion.53 = (f32[32,128]{1,0:T(8,128)S(1)}, f32[128,128,32]{1,0,2:T(8,128)S(1)}) fusion(pred[128,128]{0,1:T(8,128)(4,1)S(1)} %and_and_fusion.3, bf16[128,32,576]{0,2,1:T(8,128)(2,1)} %get-tuple-element.406, bf16[128,576]{1,0:T(8,128)(2,1)S(1)} %reshape.320), kind=kOutput, calls=%fused_computation.4.clone.1 | convolution fusion | flops 605548544 | bytes 6995968 | tf_op jit(solution)/shard_map/while/body/eval_jaxpr/thc,sc->hts/dot_general | solution.py:99
  71.6 2.7 %multiply_add_fusion.5 = f32[32,128,512]{2,1,0:T(8,128)S(1)} fusion(f32[32,128,512]{2,1,0:T(8,128)S(1)} %copy-done.1, f32[32,128]{1,0:T(8,128)S(1)} %get-tuple-element.373, f32[128,128,32]{1,0,2:T(8,128)S(1)} %get-tuple-element.371, f32[32,128]{1,0:T(8,128)S(1)} %max.11, pred[128,128]{0,1:T(8,128)(4,1)S(1)} %and_and_fusion.3, ...), kind=kOutput, calls=%fused_computation.1.clone.1 | convolution fusion | flops 543686656 | bytes 19054592 | tf_op jit(solution)/shard_map/while/body/eval_jaxpr/hts,sr->htr/dot_general | solution.py:107
  74.4 3.2 %copy-done.2 = f32[32,128,512]{2,1,0:T(8,128)} copy-done((f32[32,128,512]{2,1,0:T(8,128)}, f32[32,128,512]{2,1,0:T(8,128)S(1)}, u32[]{:S(2)}) %copy-start.2) | copy-done | bytes 8388632 | tf_op jit(solution)/shard_map/while
  77.6 1.9 %collective-permute-start = (bf16[576,128]{1,0:T(8,128)(2,1)S(1)}, bf16[576,128]{1,0:T(8,128)(2,1)S(1)}, u32[]{:S(2)}, u32[]{:S(2)}) collective-permute-start(bf16[576,128]{1,0:T(8,128)(2,1)S(1)} %get-tuple-element.390), channel_id=1, source_target_pairs={{0,2},{2,4},{4,6},{6,8},{8,10},{10,12},{12,14},{14,16},{16,18},{18... | collective-permute-start | bytes 442376 | tf_op jit(solution)/shard_map/while/body/eval_jaxpr/ppermute | solution.py:16
  79.7 5.2 %collective-permute-done = bf16[576,128]{1,0:T(8,128)(2,1)S(1)} collective-permute-done((bf16[576,128]{1,0:T(8,128)(2,1)S(1)}, bf16[576,128]{1,0:T(8,128)(2,1)S(1)}, u32[]{:S(2)}, u32[]{:S(2)}) %collective-permute-start) | collective-permute-done | bytes 147488 | tf_op jit(solution)/shard_map/while/body/eval_jaxpr/ppermute | solution.py:16
  85.1 3.6 %fusion.53 = (f32[32,128]{1,0:T(8,128)S(1)}, f32[128,128,32]{1,0,2:T(8,128)S(1)}) fusion(pred[128,128]{0,1:T(8,128)(4,1)S(1)} %and_and_fusion.3, bf16[128,32,576]{0,2,1:T(8,128)(2,1)} %get-tuple-element.406, bf16[128,576]{1,0:T(8,128)(2,1)S(1)} %reshape.320), kind=kOutput, calls=%fused_computation.4.clone.1 | convolution fusion | flops 605548544 | bytes 6995968 | tf_op jit(solution)/shard_map/while/body/eval_jaxpr/thc,sc->hts/dot_general | solution.py:99
  89.9 2.7 %multiply_add_fusion.5 = f32[32,128,512]{2,1,0:T(8,128)S(1)} fusion(f32[32,128,512]{2,1,0:T(8,128)S(1)} %copy-done.1, f32[32,128]{1,0:T(8,128)S(1)} %get-tuple-element.373, f32[128,128,32]{1,0,2:T(8,128)S(1)} %get-tuple-element.371, f32[32,128]{1,0:T(8,128)S(1)} %max.11, pred[128,128]{0,1:T(8,128)(4,1)S(1)} %and_and_fusion.3, ...), kind=kOutput, calls=%fused_computation.1.clone.1 | convolution fusion | flops 543686656 | bytes 19054592 | tf_op jit(solution)/shard_map/while/body/eval_jaxpr/hts,sr->htr/dot_general | solution.py:107
  92.7 3.2 %copy-done.2 = f32[32,128,512]{2,1,0:T(8,128)} copy-done((f32[32,128,512]{2,1,0:T(8,128)}, f32[32,128,512]{2,1,0:T(8,128)S(1)}, u32[]{:S(2)}) %copy-start.2) | copy-done | bytes 8388632 | tf_op jit(solution)/shard_map/while
  95.9 1.9 %collective-permute-start = (bf16[576,128]{1,0:T(8,128)(2,1)S(1)}, bf16[576,128]{1,0:T(8,128)(2,1)S(1)}, u32[]{:S(2)}, u32[]{:S(2)}) collective-permute-start(bf16[576,128]{1,0:T(8,128)(2,1)S(1)} %get-tuple-element.390), channel_id=1, source_target_pairs={{0,2},{2,4},{4,6},{6,8},{8,10},{10,12},{12,14},{14,16},{16,18},{18... | collective-permute-start | bytes 442376 | tf_op jit(solution)/shard_map/while/body/eval_jaxpr/ppermute | solution.py:16
  98.0 5.2 %collective-permute-done = bf16[576,128]{1,0:T(8,128)(2,1)S(1)} collective-permute-done((bf16[576,128]{1,0:T(8,128)(2,1)S(1)}, bf16[576,128]{1,0:T(8,128)(2,1)S(1)}, u32[]{:S(2)}, u32[]{:S(2)}) %collective-permute-start) | collective-permute-done | bytes 147488 | tf_op jit(solution)/shard_map/while/body/eval_jaxpr/ppermute | solution.py:16
  103.4 3.6 %fusion.53 = (f32[32,128]{1,0:T(8,128)S(1)}, f32[128,128,32]{1,0,2:T(8,128)S(1)}) fusion(pred[128,128]{0,1:T(8,128)(4,1)S(1)} %and_and_fusion.3, bf16[128,32,576]{0,2,1:T(8,128)(2,1)} %get-tuple-element.406, bf16[128,576]{1,0:T(8,128)(2,1)S(1)} %reshape.320), kind=kOutput, calls=%fused_computation.4.clone.1 | convolution fusion | flops 605548544 | bytes 6995968 | tf_op jit(solution)/shard_map/while/body/eval_jaxpr/thc,sc->hts/dot_general | solution.py:99
  108.2 2.7 %multiply_add_fusion.5 = f32[32,128,512]{2,1,0:T(8,128)S(1)} fusion(f32[32,128,512]{2,1,0:T(8,128)S(1)} %copy-done.1, f32[32,128]{1,0:T(8,128)S(1)} %get-tuple-element.373, f32[128,128,32]{1,0,2:T(8,128)S(1)} %get-tuple-element.371, f32[32,128]{1,0:T(8,128)S(1)} %max.11, pred[128,128]{0,1:T(8,128)(4,1)S(1)} %and_and_fusion.3, ...), kind=kOutput, calls=%fused_computation.1.clone.1 | convolution fusion | flops 543686656 | bytes 19054592 | tf_op jit(solution)/shard_map/while/body/eval_jaxpr/hts,sr->htr/dot_general | solution.py:107
  110.9 3.2 %copy-done.2 = f32[32,128,512]{2,1,0:T(8,128)} copy-done((f32[32,128,512]{2,1,0:T(8,128)}, f32[32,128,512]{2,1,0:T(8,128)S(1)}, u32[]{:S(2)}) %copy-start.2) | copy-done | bytes 8388632 | tf_op jit(solution)/shard_map/while
  114.1 1.9 %collective-permute-start = (bf16[576,128]{1,0:T(8,128)(2,1)S(1)}, bf16[576,128]{1,0:T(8,128)(2,1)S(1)}, u32[]{:S(2)}, u32[]{:S(2)}) collective-permute-start(bf16[576,128]{1,0:T(8,128)(2,1)S(1)} %get-tuple-element.390), channel_id=1, source_target_pairs={{0,2},{2,4},{4,6},{6,8},{8,10},{10,12},{12,14},{14,16},{16,18},{18... | collective-permute-start | bytes 442376 | tf_op jit(solution)/shard_map/while/body/eval_jaxpr/ppermute | solution.py:16
  116.3 5.2 %collective-permute-done = bf16[576,128]{1,0:T(8,128)(2,1)S(1)} collective-permute-done((bf16[576,128]{1,0:T(8,128)(2,1)S(1)}, bf16[576,128]{1,0:T(8,128)(2,1)S(1)}, u32[]{:S(2)}, u32[]{:S(2)}) %collective-permute-start) | collective-permute-done | bytes 147488 | tf_op jit(solution)/shard_map/while/body/eval_jaxpr/ppermute | solution.py:16
  121.7 3.6 %fusion.53 = (f32[32,128]{1,0:T(8,128)S(1)}, f32[128,128,32]{1,0,2:T(8,128)S(1)}) fusion(pred[128,128]{0,1:T(8,128)(4,1)S(1)} %and_and_fusion.3, bf16[128,32,576]{0,2,1:T(8,128)(2,1)} %get-tuple-element.406, bf16[128,576]{1,0:T(8,128)(2,1)S(1)} %reshape.320), kind=kOutput, calls=%fused_computation.4.clone.1 | convolution fusion | flops 605548544 | bytes 6995968 | tf_op jit(solution)/shard_map/while/body/eval_jaxpr/thc,sc->hts/dot_general | solution.py:99
  126.4 2.7 %multiply_add_fusion.5 = f32[32,128,512]{2,1,0:T(8,128)S(1)} fusion(f32[32,128,512]{2,1,0:T(8,128)S(1)} %copy-done.1, f32[32,128]{1,0:T(8,128)S(1)} %get-tuple-element.373, f32[128,128,32]{1,0,2:T(8,128)S(1)} %get-tuple-element.371, f32[32,128]{1,0:T(8,128)S(1)} %max.11, pred[128,128]{0,1:T(8,128)(4,1)S(1)} %and_and_fusion.3, ...), kind=kOutput, calls=%fused_computation.1.clone.1 | convolution fusion | flops 543686656 | bytes 19054592 | tf_op jit(solution)/shard_map/while/body/eval_jaxpr/hts,sr->htr/dot_general | solution.py:107
  129.2 3.2 %copy-done.2 = f32[32,128,512]{2,1,0:T(8,128)} copy-done((f32[32,128,512]{2,1,0:T(8,128)}, f32[32,128,512]{2,1,0:T(8,128)S(1)}, u32[]{:S(2)}) %copy-start.2) | copy-done | bytes 8388632 | tf_op jit(solution)/shard_map/while
  132.4 1.9 %collective-permute-start = (bf16[576,128]{1,0:T(8,128)(2,1)S(1)}, bf16[576,128]{1,0:T(8,128)(2,1)S(1)}, u32[]{:S(2)}, u32[]{:S(2)}) collective-permute-start(bf16[576,128]{1,0:T(8,128)(2,1)S(1)} %get-tuple-element.390), channel_id=1, source_target_pairs={{0,2},{2,4},{4,6},{6,8},{8,10},{10,12},{12,14},{14,16},{16,18},{18... | collective-permute-start | bytes 442376 | tf_op jit(solution)/shard_map/while/body/eval_jaxpr/ppermute | solution.py:16
  134.6 5.2 %collective-permute-done = bf16[576,128]{1,0:T(8,128)(2,1)S(1)} collective-permute-done((bf16[576,128]{1,0:T(8,128)(2,1)S(1)}, bf16[576,128]{1,0:T(8,128)(2,1)S(1)}, u32[]{:S(2)}, u32[]{:S(2)}) %collective-permute-start) | collective-permute-done | bytes 147488 | tf_op jit(solution)/shard_map/while/body/eval_jaxpr/ppermute | solution.py:16
  139.9 3.6 %fusion.53 = (f32[32,128]{1,0:T(8,128)S(1)}, f32[128,128,32]{1,0,2:T(8,128)S(1)}) fusion(pred[128,128]{0,1:T(8,128)(4,1)S(1)} %and_and_fusion.3, bf16[128,32,576]{0,2,1:T(8,128)(2,1)} %get-tuple-element.406, bf16[128,576]{1,0:T(8,128)(2,1)S(1)} %reshape.320), kind=kOutput, calls=%fused_computation.4.clone.1 | convolution fusion | flops 605548544 | bytes 6995968 | tf_op jit(solution)/shard_map/while/body/eval_jaxpr/thc,sc->hts/dot_general | solution.py:99
  144.7 2.7 %multiply_add_fusion.5 = f32[32,128,512]{2,1,0:T(8,128)S(1)} fusion(f32[32,128,512]{2,1,0:T(8,128)S(1)} %copy-done.1, f32[32,128]{1,0:T(8,128)S(1)} %get-tuple-element.373, f32[128,128,32]{1,0,2:T(8,128)S(1)} %get-tuple-element.371, f32[32,128]{1,0:T(8,128)S(1)} %max.11, pred[128,128]{0,1:T(8,128)(4,1)S(1)} %and_and_fusion.3, ...), kind=kOutput, calls=%fused_computation.1.clone.1 | convolution fusion | flops 543686656 | bytes 19054592 | tf_op jit(solution)/shard_map/while/body/eval_jaxpr/hts,sr->htr/dot_general | solution.py:107
  147.5 3.2 %copy-done.2 = f32[32,128,512]{2,1,0:T(8,128)} copy-done((f32[32,128,512]{2,1,0:T(8,128)}, f32[32,128,512]{2,1,0:T(8,128)S(1)}, u32[]{:S(2)}) %copy-start.2) | copy-done | bytes 8388632 | tf_op jit(solution)/shard_map/while
  150.7 6.5 %fusion.18 = bf16[32,128,128]{1,2,0:T(8,128)(2,1)S(1)} fusion(bf16[32,512,128]{2,1,0:T(8,128)(2,1)} %param.14, f32[32,128,512]{2,1,0:T(8,128)} %get-tuple-element.240, f32[32,128]{1,0:T(8,128)S(1)} %get-tuple-element.241), kind=kOutput, calls=%fused_computation.33 | convolution fusion | flops 541589504 | bytes 13647872 | tf_op jit(solution)/shard_map/htr,hrv->thv/dot_general | solution.py:135
  157.3 1.3 copy.55
  (115 shorter events, 12.9 us)
Async XLA Ops:
  0.0 11.1 %copy-start = (bf16[128,4096]{1,0:T(8,128)(2,1)S(1)}, bf16[128,4096]{1,0:T(8,128)(2,1)}, u32[]{:S(2)}) copy-start(bf16[128,4096]{1,0:T(8,128)(2,1)} %param.11) | copy-start | bytes 3145732
  22.7 7.3 %collective-permute-start = (bf16[576,128]{1,0:T(8,128)(2,1)S(1)}, bf16[576,128]{1,0:T(8,128)(2,1)S(1)}, u32[]{:S(2)}, u32[]{:S(2)}) collective-permute-start(bf16[576,128]{1,0:T(8,128)(2,1)S(1)} %get-tuple-element.390), channel_id=1, source_target_pairs={{0,2},{2,4},{4,6},{6,8},{8,10},{10,12},{12,14},{14,16},{16,18},{18... | collective-permute-start | bytes 442376 | tf_op jit(solution)/shard_map/while/body/eval_jaxpr/ppermute | solution.py:16
  30.2 4.8 %copy-start.1 = (f32[32,128,512]{2,1,0:T(8,128)S(1)}, f32[32,128,512]{2,1,0:T(8,128)}, u32[]{:S(2)}) copy-start(f32[32,128,512]{2,1,0:T(8,128)} %get-tuple-element.389) | copy-start | bytes 25165828 | tf_op jit(solution)/shard_map/while
  37.8 3.2 %copy-start.2 = (f32[32,128,512]{2,1,0:T(8,128)}, f32[32,128,512]{2,1,0:T(8,128)S(1)}, u32[]{:S(2)}) copy-start(f32[32,128,512]{2,1,0:T(8,128)S(1)} %multiply_add_fusion.5) | copy-start | bytes 25165828 | tf_op jit(solution)/shard_map/while
  41.0 7.3 %collective-permute-start = (bf16[576,128]{1,0:T(8,128)(2,1)S(1)}, bf16[576,128]{1,0:T(8,128)(2,1)S(1)}, u32[]{:S(2)}, u32[]{:S(2)}) collective-permute-start(bf16[576,128]{1,0:T(8,128)(2,1)S(1)} %get-tuple-element.390), channel_id=1, source_target_pairs={{0,2},{2,4},{4,6},{6,8},{8,10},{10,12},{12,14},{14,16},{16,18},{18... | collective-permute-start | bytes 442376 | tf_op jit(solution)/shard_map/while/body/eval_jaxpr/ppermute | solution.py:16
  48.5 4.8 %copy-start.1 = (f32[32,128,512]{2,1,0:T(8,128)S(1)}, f32[32,128,512]{2,1,0:T(8,128)}, u32[]{:S(2)}) copy-start(f32[32,128,512]{2,1,0:T(8,128)} %get-tuple-element.389) | copy-start | bytes 25165828 | tf_op jit(solution)/shard_map/while
  56.1 3.2 %copy-start.2 = (f32[32,128,512]{2,1,0:T(8,128)}, f32[32,128,512]{2,1,0:T(8,128)S(1)}, u32[]{:S(2)}) copy-start(f32[32,128,512]{2,1,0:T(8,128)S(1)} %multiply_add_fusion.5) | copy-start | bytes 25165828 | tf_op jit(solution)/shard_map/while
  59.3 7.3 %collective-permute-start = (bf16[576,128]{1,0:T(8,128)(2,1)S(1)}, bf16[576,128]{1,0:T(8,128)(2,1)S(1)}, u32[]{:S(2)}, u32[]{:S(2)}) collective-permute-start(bf16[576,128]{1,0:T(8,128)(2,1)S(1)} %get-tuple-element.390), channel_id=1, source_target_pairs={{0,2},{2,4},{4,6},{6,8},{8,10},{10,12},{12,14},{14,16},{16,18},{18... | collective-permute-start | bytes 442376 | tf_op jit(solution)/shard_map/while/body/eval_jaxpr/ppermute | solution.py:16
  66.8 4.8 %copy-start.1 = (f32[32,128,512]{2,1,0:T(8,128)S(1)}, f32[32,128,512]{2,1,0:T(8,128)}, u32[]{:S(2)}) copy-start(f32[32,128,512]{2,1,0:T(8,128)} %get-tuple-element.389) | copy-start | bytes 25165828 | tf_op jit(solution)/shard_map/while
  74.3 3.2 %copy-start.2 = (f32[32,128,512]{2,1,0:T(8,128)}, f32[32,128,512]{2,1,0:T(8,128)S(1)}, u32[]{:S(2)}) copy-start(f32[32,128,512]{2,1,0:T(8,128)S(1)} %multiply_add_fusion.5) | copy-start | bytes 25165828 | tf_op jit(solution)/shard_map/while
  77.6 7.3 %collective-permute-start = (bf16[576,128]{1,0:T(8,128)(2,1)S(1)}, bf16[576,128]{1,0:T(8,128)(2,1)S(1)}, u32[]{:S(2)}, u32[]{:S(2)}) collective-permute-start(bf16[576,128]{1,0:T(8,128)(2,1)S(1)} %get-tuple-element.390), channel_id=1, source_target_pairs={{0,2},{2,4},{4,6},{6,8},{8,10},{10,12},{12,14},{14,16},{16,18},{18... | collective-permute-start | bytes 442376 | tf_op jit(solution)/shard_map/while/body/eval_jaxpr/ppermute | solution.py:16
  85.1 4.8 %copy-start.1 = (f32[32,128,512]{2,1,0:T(8,128)S(1)}, f32[32,128,512]{2,1,0:T(8,128)}, u32[]{:S(2)}) copy-start(f32[32,128,512]{2,1,0:T(8,128)} %get-tuple-element.389) | copy-start | bytes 25165828 | tf_op jit(solution)/shard_map/while
  92.6 3.2 %copy-start.2 = (f32[32,128,512]{2,1,0:T(8,128)}, f32[32,128,512]{2,1,0:T(8,128)S(1)}, u32[]{:S(2)}) copy-start(f32[32,128,512]{2,1,0:T(8,128)S(1)} %multiply_add_fusion.5) | copy-start | bytes 25165828 | tf_op jit(solution)/shard_map/while
  95.9 7.3 %collective-permute-start = (bf16[576,128]{1,0:T(8,128)(2,1)S(1)}, bf16[576,128]{1,0:T(8,128)(2,1)S(1)}, u32[]{:S(2)}, u32[]{:S(2)}) collective-permute-start(bf16[576,128]{1,0:T(8,128)(2,1)S(1)} %get-tuple-element.390), channel_id=1, source_target_pairs={{0,2},{2,4},{4,6},{6,8},{8,10},{10,12},{12,14},{14,16},{16,18},{18... | collective-permute-start | bytes 442376 | tf_op jit(solution)/shard_map/while/body/eval_jaxpr/ppermute | solution.py:16
  103.4 4.8 %copy-start.1 = (f32[32,128,512]{2,1,0:T(8,128)S(1)}, f32[32,128,512]{2,1,0:T(8,128)}, u32[]{:S(2)}) copy-start(f32[32,128,512]{2,1,0:T(8,128)} %get-tuple-element.389) | copy-start | bytes 25165828 | tf_op jit(solution)/shard_map/while
  110.9 3.2 %copy-start.2 = (f32[32,128,512]{2,1,0:T(8,128)}, f32[32,128,512]{2,1,0:T(8,128)S(1)}, u32[]{:S(2)}) copy-start(f32[32,128,512]{2,1,0:T(8,128)S(1)} %multiply_add_fusion.5) | copy-start | bytes 25165828 | tf_op jit(solution)/shard_map/while
  114.1 7.3 %collective-permute-start = (bf16[576,128]{1,0:T(8,128)(2,1)S(1)}, bf16[576,128]{1,0:T(8,128)(2,1)S(1)}, u32[]{:S(2)}, u32[]{:S(2)}) collective-permute-start(bf16[576,128]{1,0:T(8,128)(2,1)S(1)} %get-tuple-element.390), channel_id=1, source_target_pairs={{0,2},{2,4},{4,6},{6,8},{8,10},{10,12},{12,14},{14,16},{16,18},{18... | collective-permute-start | bytes 442376 | tf_op jit(solution)/shard_map/while/body/eval_jaxpr/ppermute | solution.py:16
  121.6 4.8 %copy-start.1 = (f32[32,128,512]{2,1,0:T(8,128)S(1)}, f32[32,128,512]{2,1,0:T(8,128)}, u32[]{:S(2)}) copy-start(f32[32,128,512]{2,1,0:T(8,128)} %get-tuple-element.389) | copy-start | bytes 25165828 | tf_op jit(solution)/shard_map/while
  129.2 3.2 %copy-start.2 = (f32[32,128,512]{2,1,0:T(8,128)}, f32[32,128,512]{2,1,0:T(8,128)S(1)}, u32[]{:S(2)}) copy-start(f32[32,128,512]{2,1,0:T(8,128)S(1)} %multiply_add_fusion.5) | copy-start | bytes 25165828 | tf_op jit(solution)/shard_map/while
  132.4 7.3 %collective-permute-start = (bf16[576,128]{1,0:T(8,128)(2,1)S(1)}, bf16[576,128]{1,0:T(8,128)(2,1)S(1)}, u32[]{:S(2)}, u32[]{:S(2)}) collective-permute-start(bf16[576,128]{1,0:T(8,128)(2,1)S(1)} %get-tuple-element.390), channel_id=1, source_target_pairs={{0,2},{2,4},{4,6},{6,8},{8,10},{10,12},{12,14},{14,16},{16,18},{18... | collective-permute-start | bytes 442376 | tf_op jit(solution)/shard_map/while/body/eval_jaxpr/ppermute | solution.py:16
  139.9 4.8 %copy-start.1 = (f32[32,128,512]{2,1,0:T(8,128)S(1)}, f32[32,128,512]{2,1,0:T(8,128)}, u32[]{:S(2)}) copy-start(f32[32,128,512]{2,1,0:T(8,128)} %get-tuple-element.389) | copy-start | bytes 25165828 | tf_op jit(solution)/shard_map/while
  147.5 3.2 %copy-start.2 = (f32[32,128,512]{2,1,0:T(8,128)}, f32[32,128,512]{2,1,0:T(8,128)S(1)}, u32[]{:S(2)}) copy-start(f32[32,128,512]{2,1,0:T(8,128)S(1)} %multiply_add_fusion.5) | copy-start | bytes 25165828 | tf_op jit(solution)/shard_map/while
where the time goes:
time: 159 us
  matrix products  59.4 us (37%)
  waiting for transfers between devices  36.4 us (23%)
  local copies, waits for them, and re-layouts  31.8 us (20%)
  starting transfers between devices  13.4 us (8%)
  other arithmetic  11.7 us (7%)
  blocking collectives  5.03 us (3%)
    ppermute x7, waiting for transfers between devices, shifted(): lax.ppermute(value, axis, [(source, source + steps) for source in range(l...  36.4 us
    while x42, local copies, waits for them, and re-layouts  26.7 us
    dot_general x8, matrix products, attend(): jnp.einsum('thc,sc->hts', queries, key_block, preferred_element_type=jnp....  26.1 us
    dot_general x8, matrix products, attend(): jnp.einsum('hts,sr->htr', weights.astype(jnp.bfloat16), key_block[:, :lat...  23.2 us
    ppermute x7, starting transfers between devices, shifted(): lax.ppermute(value, axis, [(source, source + steps) for source in range(l...  13.4 us
    dot_general x1, matrix products, shards(): jnp.einsum('htr,hrv->thv', mixed_latent, value_up, preferred_element_type...  6.55 us
    all_gather x1, blocking collectives, shards(): lax.all_gather(kv_half.reshape(-1, 128), 'head', axis=0, tiled=True)  5.03 us
    reduce_sum x8, other arithmetic, attend(): new_total = running_total * factor + jnp.sum(weights, axis=2)  4.45 us
  transfers between devices with their start and end apart: 7, of which 7 were waited for; matrix products, arithmetic and copies ran while one was open for 1% of the time, Pallas kernels for 0%

commit v1 on v0

v1 whole, which is shorter than its diff:
```python
import functools

import jax
import jax.numpy as jnp
import numpy as np
from jax import lax
from jax.experimental import pallas as pl
from jax.experimental.pallas import tpu as pltpu
from jax.sharding import PartitionSpec as P

epsilon = 1e-06
masked_score = -1e30
PLANE = 4
GROUP = 8
SUB = 4
VMEM = pl.BlockSpec(memory_space=pltpu.VMEM)
SMEM = pl.BlockSpec(memory_space=pltpu.SMEM)


def begin_of(positions, lengths_ref):
    begin = jnp.zeros_like(positions)
    start = jnp.int32(0)
    for doc in range(lengths_ref.shape[0] - 1):
        start = start + lengths_ref[doc]
        begin = jnp.where(positions >= start, start, begin)
    return begin


def half_start(plane, flip_y, flip_core, flip_head, block_rows, half_rows):
    ctx = lax.axis_index("ctx")
    head = lax.axis_index("head")
    core = lax.rem(ctx, 2)
    row = lax.rem(ctx // 2, 2)
    base = ctx // PLANE - plane
    row = 1 - row if flip_y else row
    core = 1 - core if flip_core else core
    head = 1 - head if flip_head else head
    return (base * PLANE + row * 2 + core) * block_rows + head * half_rows


def query_kernel(lengths_ref, freq_ref, qn_ref, qr_ref, ku_ref, q_ref, cos_ref, sin_ref):
    rows = qn_ref.shape[0]
    heads, nope, latent = ku_ref.shape
    rope = qr_ref.shape[1] // heads
    ctx = lax.axis_index("ctx")
    freq = freq_ref[0:1, :]
    key_rows = rows // 2
    for plane in range(3):
        first = half_start(plane, False, False, False, rows, key_rows)
        pos = first + lax.broadcasted_iota(jnp.int32, (key_rows, 128), 0)
        angle = (pos - begin_of(pos, lengths_ref)).astype(jnp.float32) * freq
        cos_ref[plane] = jnp.cos(angle)
        sin_ref[plane] = jnp.sin(angle)
    pos = ctx * rows + lax.broadcasted_iota(jnp.int32, (rows, 128), 0)
    angle = (pos - begin_of(pos, lengths_ref)).astype(jnp.float32) * freq
    lane = lax.broadcasted_iota(jnp.int32, (rows, 128), 1)
    low = lax.rem(lane, rope) < rope // 2
    cos = jnp.cos(angle)
    sin = jnp.sin(angle)
    sin = jnp.where(low, -sin, sin)

    def group(index, carry):
        for j in range(0, GROUP, 2):
            head = index * GROUP + j
            pair = qr_ref[:, pl.ds(pl.multiple_of(head * rope, 128), 128)].astype(jnp.float32)
            partner = jnp.where(low, pltpu.roll(pair, 128 - rope // 2, 1), pltpu.roll(pair, rope // 2, 1))
            rotated = pair * cos + partner * sin
            shifted = pltpu.roll(rotated, rope, 1)
            for k in range(2):
                at = pl.ds(pl.multiple_of((head + k) * rows, rows), rows)
                nope_rows = qn_ref[:, pl.ds(pl.multiple_of((head + k) * nope, 128), nope)]
                absorbed = jnp.dot(nope_rows, ku_ref[head + k], preferred_element_type=jnp.float32)
                q_ref[at, :latent] = absorbed.astype(jnp.bfloat16)
                part = rotated if k == 0 else shifted
                q_ref[at, latent:] = jnp.where(lane < rope, part, 0.0).astype(jnp.bfloat16)
        return carry

    lax.fori_loop(0, heads // GROUP, group, 0)


def rows_kernel(own_ref, one_ref, two_ref, gain_ref, cos_ref, sin_ref, rows_ref, send_ref):
    latent = gain_ref.shape[1]
    full = own_ref.shape[1]
    half = (full - latent) // 2
    row = lax.rem(lax.axis_index("ctx") // 2, 2)
    gain = gain_ref[0:1, :]
    for plane, raw_ref in enumerate((own_ref, one_ref, two_ref)):
        part = raw_ref[:, :latent].astype(jnp.float32)
        mean = jnp.mean(part * part, axis=1, keepdims=True)
        normed = part * lax.rsqrt(mean + epsilon) * gain
        rope = raw_ref[:, latent:].astype(jnp.float32)
        first, second = rope[:, :half], rope[:, half:]
        cos, sin = cos_ref[plane][:, :half], sin_ref[plane][:, :half]
        turned = jnp.concatenate([first * cos - second * sin, second * cos + first * sin], axis=1)
        rows_ref[plane, :, :latent] = normed.astype(jnp.bfloat16)
        rows_ref[plane, :, latent:] = turned.astype(jnp.bfloat16)
    send_ref[...] = rows_ref[pl.ds(row, 2)]


def attend_kernel(layout, scale, lengths_ref, q_ref, vu_ref, *refs):
    count = len(layout)
    piece_refs = refs[:count]
    out_ref, kv_ref = refs[count:]
    heads, latent, value = vu_ref.shape
    rows = q_ref.shape[0] // heads
    half_rows = rows // 2
    ctx = lax.axis_index("ctx")
    core = lax.rem(ctx, 2)
    row = lax.rem(ctx // 2, 2)
    keys = kv_ref.shape[0]
    full = piece_refs[0].shape[2]
    kv_ref[:, full:] = jnp.zeros((keys, kv_ref.shape[1] - full), jnp.bfloat16)
    lane = lax.broadcasted_iota(jnp.int32, (rows, keys), 1)
    key_pos = jnp.zeros((rows, keys), jnp.int32)
    at = 0
    for (flip_y, flip_core, flip_head), ref in zip(layout, piece_refs):
        if flip_y:
            index, plane = 0, 1 - row
        else:
            index = plane = 1 - core if flip_core else 0
        for step in range(2):
            kv_ref[at : at + half_rows, :full] = ref[index + step]
            first = half_start(plane + step, flip_y, flip_core, flip_head, rows, half_rows)
            key_pos = jnp.where(lane >= at, first + lane - at, key_pos)
            at += half_rows
    pos = ctx * rows + lax.broadcasted_iota(jnp.int32, (rows, keys), 0)
    live = (key_pos <= pos) & (key_pos >= begin_of(pos, lengths_ref))

    def scores(base):
        at = pl.ds(pl.multiple_of(base * rows, rows), SUB * rows)
        return lax.dot_general(
            q_ref[at, :], kv_ref[...], (((1,), (1,)), ((), ())), preferred_element_type=jnp.float32
        )

    def group(index, carry):
        subs = GROUP // SUB
        now = scores(index * GROUP)
        for sub in range(subs):
            base = index * GROUP + sub * SUB
            later = scores(base + SUB) if sub + 1 < subs else None
            now = jnp.where(live[None], now.reshape(SUB, rows, keys) * scale, masked_score)
            most = jnp.max(now, axis=2, keepdims=True)
            weights = jnp.exp(now - most)
            total = jnp.sum(weights, axis=2, keepdims=True).reshape(SUB * rows, 1)
            mixed = jnp.dot(
                weights.astype(jnp.bfloat16).reshape(SUB * rows, keys),
                kv_ref[:, :latent],
                preferred_element_type=jnp.float32,
            )
            mixed = (mixed / total).astype(jnp.bfloat16)
            for j in range(SUB):
                result = jnp.dot(
                    mixed[j * rows : (j + 1) * rows], vu_ref[base + j], preferred_element_type=jnp.float32
                )
                out_ref[:, pl.ds(pl.multiple_of((base + j) * value, 128), value)] = result.astype(jnp.bfloat16)
            now = later
        return carry

    lax.fori_loop(0, heads // GROUP, group, 0)


def params():
    return pltpu.CompilerParams(vmem_limit_bytes=48 * 2**20)


def shards(latent_raw, kv_gain, query_nope, query_rope, key_up, value_up, doc_lengths):
    rows = query_nope.shape[0]
    heads, nope, latent = key_up.shape
    value = value_up.shape[2]
    half_rows, full = latent_raw.shape
    rope = full - latent
    wide = latent + 128
    ctx_size = lax.axis_size("ctx")
    scale = (nope + rope) ** (-0.5)

    def plane_shift(array, planes):
        steps = planes * PLANE
        return lax.ppermute(array, "ctx", [(s, (s + steps) % ctx_size) for s in range(ctx_size)])

    def swap_ctx(array, bit):
        return lax.ppermute(array, "ctx", [(s, s ^ bit) for s in range(ctx_size)])

    def swap_head(array):
        return lax.ppermute(array, "head", [(0, 1), (1, 0)])

    one = plane_shift(latent_raw, 1)
    two = plane_shift(latent_raw, 2)
    freq = np.float32(10000.0) ** (np.float32(-2.0) * np.arange(rope // 2, dtype=np.float32) / np.float32(rope))
    freq = jnp.asarray(np.tile(freq.astype(np.float32), (8, 128 // (rope // 2))))
    table = jax.ShapeDtypeStruct((3, half_rows, 128), jnp.float32)
    queries, cos, sin = pl.pallas_call(
        query_kernel,
        out_shape=(jax.ShapeDtypeStruct((heads * rows, wide), jnp.bfloat16), table, table),
        in_specs=[SMEM] + [VMEM] * 4,
        out_specs=[VMEM] * 3,
        compiler_params=params(),
        cost_estimate=pl.CostEstimate(
            flops=2 * heads * rows * nope * latent, bytes_accessed=8 * 2**20, transcendentals=0
        ),
        name="queries",
    )(doc_lengths, freq, query_nope, query_rope, key_up)
    near, send = pl.pallas_call(
        rows_kernel,
        out_shape=(
            jax.ShapeDtypeStruct((3, half_rows, full), jnp.bfloat16),
            jax.ShapeDtypeStruct((2, half_rows, full), jnp.bfloat16),
        ),
        in_specs=[VMEM] * 6,
        out_specs=[VMEM] * 2,
        compiler_params=params(),
        name="rows",
    )(latent_raw, one, two, kv_gain[None], cos, sin)
    across = swap_ctx(send, 2)
    side = swap_head(near)
    corner = swap_head(across)
    pieces = [near, across, side, corner]
    pieces = pieces + [swap_ctx(piece, 1) for piece in pieces]
    layout = []
    for flip_core in (False, True):
        layout += [(False, flip_core, False), (True, flip_core, False), (False, flip_core, True), (True, flip_core, True)]
    keys = 2 * half_rows * len(pieces)
    return pl.pallas_call(
        functools.partial(attend_kernel, tuple(layout), scale),
        out_shape=jax.ShapeDtypeStruct((rows, heads * value), jnp.bfloat16),
        in_specs=[SMEM] + [VMEM] * (2 + len(pieces)),
        out_specs=VMEM,
        scratch_shapes=[pltpu.VMEM((keys, wide), jnp.bfloat16)],
        compiler_params=params(),
        name="attend",
    )(doc_lengths, queries, value_up, *pieces)


def solution(mesh):
    return jax.shard_map(
        shards,
        mesh=mesh,
        in_specs=(
            P(("ctx", "head"), None),
            P(),
            P("ctx", "head"),
            P("ctx", "head"),
            P("head", None, None),
            P("head", None, None),
            P(),
        ),
        out_specs=P("ctx", "head"),
        check_vma=False,
    )
```

time: 159 us -> 49.7 us (0.31)
  the two profiles are of different devices: /device:TPU:24 before, /device:TPU:0 now
where the time goes in v1:
time: 49.7 us; the launch traced here: 49.4 us
  Pallas kernels  24.6 us (49%)
  starting transfers between devices  10.7 us (22%)
  waiting for transfers between devices  8.23 us (17%)
  local copies, waits for them, and re-layouts  5.8 us (12%)
    pallas_call x1, Pallas kernels, shards(): pl.pallas_call(functools.partial(attend_kernel, tuple(layout), scale), ou...  19 us
    unnamed x16, local copies, waits for them, and re-layouts  5.8 us
    ppermute x2, starting transfers between devices, plane_shift(): lax.ppermute(array, 'ctx', [(s, (s + steps) % ctx_size) for s in range(ct...  5.61 us
    pallas_call x1, Pallas kernels, shards(): pl.pallas_call(query_kernel, out_shape=(jax.ShapeDtypeStruct((heads * row...  5.28 us
    ppermute x2, waiting for transfers between devices, swap_head(): return lax.ppermute(array, 'head', [(0, 1), (1, 0)])  4.5 us
    ppermute x5, waiting for transfers between devices, swap_ctx(): return lax.ppermute(array, 'ctx', [(s, s ^ bit) for s in range(ctx_size)])  3.72 us
    ppermute x2, starting transfers between devices, swap_head(): return lax.ppermute(array, 'head', [(0, 1), (1, 0)])  3 us
    ppermute x5, starting transfers between devices, swap_ctx(): return lax.ppermute(array, 'ctx', [(s, s ^ bit) for s in range(ctx_size)])  2.1 us
  transfers between devices with their start and end apart: 9, of which 4 were waited for; matrix products, arithmetic and copies ran while one was open for 0% of the time, Pallas kernels for 11%

profile of v1, /device:TPU:0, one launch (start us, length us, event | category | flops | bytes accessed | tf_op | source)
XLA Modules:
  0.0 49.4 jit_solution(11648463533767161541)
XLA Ops:
  0.0 3.0 %collective-permute-start = (bf16[64,576]{1,0:T(8,128)(2,1)}, bf16[64,576]{1,0:T(8,128)(2,1)S(1)}, u32[]{:S(2)}, u32[]{:S(2)}) collective-permute-start(bf16[64,576]{1,0:T(8,128)(2,1)} %own_ref.1), channel_id=1, source_target_pairs={{0,8},{2,10},{4,12},{6,14},{8,16},{10,18},{12,20},{14,22},{16,24},... | collective-permute-start | bytes 221192 | tf_op jit(solution)/shard_map/ppermute | solution.py:178
  3.0 2.6 %collective-permute-start.1 = (bf16[64,576]{1,0:T(8,128)(2,1)}, bf16[64,576]{1,0:T(8,128)(2,1)S(1)}, u32[]{:S(2)}, u32[]{:S(2)}) collective-permute-start(bf16[64,576]{1,0:T(8,128)(2,1)} %own_ref.1), channel_id=1, source_target_pairs={{0,16},{2,18},{4,20},{6,22},{8,24},{10,26},{12,28},{14,30},{16,0},... | collective-permute-start | bytes 221192 | tf_op jit(solution)/shard_map/ppermute | solution.py:178
  5.6 0.0 copy-start
  5.6 2.2 %copy-done = bf16[32,128,512]{2,1,0:T(8,128)(2,1)S(1)} copy-done((bf16[32,128,512]{2,1,0:T(8,128)(2,1)S(1)}, bf16[32,128,512]{2,1,0:T(8,128)(2,1)}, u32[]{:S(2)}) %copy-start) | copy-done | bytes 4194328
  7.8 0.0 copy-start.2
  7.8 1.2 %copy-done.2 = bf16[128,4096]{1,0:T(8,128)(2,1)S(1)} copy-done((bf16[128,4096]{1,0:T(8,128)(2,1)S(1)}, bf16[128,4096]{1,0:T(8,128)(2,1)}, u32[]{:S(2)}) %copy-start.2) | copy-done | bytes 1048600
  9.0 0.0 copy-start.3
  9.0 1.0 %copy-done.3 = bf16[128,2048]{1,0:T(8,128)(2,1)S(1)} copy-done((bf16[128,2048]{1,0:T(8,128)(2,1)S(1)}, bf16[128,2048]{1,0:T(8,128)(2,1)}, u32[]{:S(2)}) %copy-start.3) | copy-done | bytes 524312
  10.1 0.0 copy-start.5
  10.1 0.7 %copy-done.5 = f32[8,128]{1,0:T(8,128)S(1)} copy-done((f32[8,128]{1,0:T(8,128)S(1)}, f32[8,128]{1,0:T(8,128)}, u32[]{:S(2)}) %copy-start.5) | copy-done | bytes 4120
  10.8 0.0 copy-start.7
  10.8 0.7 %copy-done.7 = s32[4]{0:T(128)S(1)} copy-done((s32[4]{0:T(128)S(1)}, s32[4]{0:T(128)}, u32[]{:S(2)}) %copy-start.7) | copy-done | bytes 40
  11.4 0.0 copy-start.4
  11.4 0.0 copy-start.6
  11.4 0.0 copy-start.1
  11.4 5.3 %queries.1 = (bf16[4096,640]{1,0:T(8,128)(2,1)}, f32[3,64,128]{2,1,0:T(8,128)S(1)}, f32[3,64,128]{2,1,0:T(8,128)S(1)}) custom-call(s32[4]{0:T(128)S(1)} %copy-done.7, f32[8,128]{1,0:T(8,128)S(1)} %copy-done.5, bf16[128,4096]{1,0:T(8,128)(2,1)S(1)} %copy-done.2, bf16[128,2048]{1,0:T(8,128)(2,1)S(1)} %copy-done.3, bf16[32,128,512]{2,1,0:T(8,128)(2,1)S(1)} %copy-done), custom_call_target="tpu_custom_call" | custom-call | flops 536870912 | bytes 8388608 | tf_op jit(solution)/shard_map/queries/pallas_call | solution.py:191
  16.7 0.0 collective-permute-done.one_ref
  16.7 0.0 collective-permute-done.1.two_ref
  16.7 0.0 copy-done.4
  16.7 0.0 copy-done.6
  16.7 0.4 rows.1
  17.1 1.6 %collective-permute-start.2 = (bf16[2,64,576]{2,1,0:T(8,128)(2,1)S(1)}, bf16[2,64,576]{2,1,0:T(8,128)(2,1)S(1)}, u32[]{:S(2)}, u32[]{:S(2)}) collective-permute-start(bf16[2,64,576]{2,1,0:T(8,128)(2,1)S(1)} %get-tuple-element.14), channel_id=1, source_target_pairs={{0,4},{2,6},{4,0},{6,2},{8,12},{10,14},{12,8},{14,10},{16,20},{18,... | collective-permute-start | bytes 442376 | tf_op jit(solution)/shard_map/ppermute | solution.py:181
  18.7 1.5 %collective-permute-start.3 = (bf16[3,64,576]{2,1,0:T(8,128)(2,1)S(1)}, bf16[3,64,576]{2,1,0:T(8,128)(2,1)S(1)}, u32[]{:S(2)}, u32[]{:S(2)}) collective-permute-start(bf16[3,64,576]{2,1,0:T(8,128)(2,1)S(1)} %get-tuple-element.13.refs_0_), channel_id=1, source_target_pairs={{0,1},{1,0},{2,3},{3,2},{4,5},{5,4},{6,7},{7,6},{8,9},{9,8},{10,11... | collective-permute-start | bytes 663560 | tf_op jit(solution)/shard_map/ppermute | solution.py:184
  20.2 2.3 %collective-permute-done.2.refs_1_ = bf16[2,64,576]{2,1,0:T(8,128)(2,1)S(1)} collective-permute-done((bf16[2,64,576]{2,1,0:T(8,128)(2,1)S(1)}, bf16[2,64,576]{2,1,0:T(8,128)(2,1)S(1)}, u32[]{:S(2)}, u32[]{:S(2)}) %collective-permute-start.2) | collective-permute-done | bytes 147488 | tf_op jit(solution)/shard_map/ppermute | solution.py:181
  22.5 1.5 %collective-permute-start.4 = (bf16[2,64,576]{2,1,0:T(8,128)(2,1)S(1)}, bf16[2,64,576]{2,1,0:T(8,128)(2,1)S(1)}, u32[]{:S(2)}, u32[]{:S(2)}) collective-permute-start(bf16[2,64,576]{2,1,0:T(8,128)(2,1)S(1)} %collective-permute-done.2.refs_1_), channel_id=1, source_target_pairs={{0,1},{1,0},{2,3},{3,2},{4,5},{5,4},{6,7},{7,6},{8,9},{9,8},{10,11... | collective-permute-start | bytes 442376 | tf_op jit(solution)/shard_map/ppermute | solution.py:184
  24.0 0.0 collective-permute-start.5
  24.0 3.3 %collective-permute-done.3.refs_2_ = bf16[3,64,576]{2,1,0:T(8,128)(2,1)S(1)} collective-permute-done((bf16[3,64,576]{2,1,0:T(8,128)(2,1)S(1)}, bf16[3,64,576]{2,1,0:T(8,128)(2,1)S(1)}, u32[]{:S(2)}, u32[]{:S(2)}) %collective-permute-start.3) | collective-permute-done | bytes 221216 | tf_op jit(solution)/shard_map/ppermute | solution.py:184
  27.3 0.0 collective-permute-start.7
  27.3 0.5 %collective-permute-start.6 = (bf16[2,64,576]{2,1,0:T(8,128)(2,1)S(1)}, bf16[2,64,576]{2,1,0:T(8,128)(2,1)S(1)}, u32[]{:S(2)}, u32[]{:S(2)}) collective-permute-start(bf16[2,64,576]{2,1,0:T(8,128)(2,1)S(1)} %collective-permute-done.2.refs_1_), channel_id=1, source_target_pairs={{0,2},{2,0},{4,6},{6,4},{8,10},{10,8},{12,14},{14,12},{16,18},{18,... | collective-permute-start | bytes 442376 | tf_op jit(solution)/shard_map/ppermute | solution.py:181
  27.8 1.2 %collective-permute-done.4.refs_3_ = bf16[2,64,576]{2,1,0:T(8,128)(2,1)S(1)} collective-permute-done((bf16[2,64,576]{2,1,0:T(8,128)(2,1)S(1)}, bf16[2,64,576]{2,1,0:T(8,128)(2,1)S(1)}, u32[]{:S(2)}, u32[]{:S(2)}) %collective-permute-start.4) | collective-permute-done | bytes 147488 | tf_op jit(solution)/shard_map/ppermute | solution.py:184
  29.0 0.0 collective-permute-start.8
  29.1 0.0 collective-permute-done.5.refs_4_
  29.1 0.0 collective-permute-done.6.refs_5_
  29.1 1.4 %collective-permute-done.8.refs_7_ = bf16[2,64,576]{2,1,0:T(8,128)(2,1)S(1)} collective-permute-done((bf16[2,64,576]{2,1,0:T(8,128)(2,1)S(1)}, bf16[2,64,576]{2,1,0:T(8,128)(2,1)S(1)}, u32[]{:S(2)}, u32[]{:S(2)}) %collective-permute-start.8) | collective-permute-done | bytes 147488 | tf_op jit(solution)/shard_map/ppermute | solution.py:181
  30.4 0.0 collective-permute-done.7.refs_6_
  30.4 0.0 copy-done.1
  30.4 19.0 %attend.1 = bf16[128,4096]{1,0:T(8,128)(2,1)} custom-call(s32[4]{0:T(128)S(1)} %copy-done.7, bf16[4096,640]{1,0:T(8,128)(2,1)} %get-tuple-element.10.q_ref, bf16[32,512,128]{2,1,0:T(8,128)(2,1)S(1)} %copy-done.1, bf16[3,64,576]{2,1,0:T(8,128)(2,1)S(1)} %get-tuple-element.13.refs_0_, bf16[2,64,576]{2,1,0:T(8,128)(2,1)S(1)} %collective-permute-done.2.refs_1_, ...), custom_call_target="tpu_custom_call" | custom-call | tf_op jit(solution)/shard_map/attend/pallas_call | solution.py:222
Async XLA Ops:
  0.0 16.7 %collective-permute-start = (bf16[64,576]{1,0:T(8,128)(2,1)}, bf16[64,576]{1,0:T(8,128)(2,1)S(1)}, u32[]{:S(2)}, u32[]{:S(2)}) collective-permute-start(bf16[64,576]{1,0:T(8,128)(2,1)} %own_ref.1), channel_id=1, source_target_pairs={{0,8},{2,10},{4,12},{6,14},{8,16},{10,18},{12,20},{14,22},{16,24},... | collective-permute-start | bytes 221192 | tf_op jit(solution)/shard_map/ppermute | solution.py:178
  3.0 13.7 %collective-permute-start.1 = (bf16[64,576]{1,0:T(8,128)(2,1)}, bf16[64,576]{1,0:T(8,128)(2,1)S(1)}, u32[]{:S(2)}, u32[]{:S(2)}) collective-permute-start(bf16[64,576]{1,0:T(8,128)(2,1)} %own_ref.1), channel_id=1, source_target_pairs={{0,16},{2,18},{4,20},{6,22},{8,24},{10,26},{12,28},{14,30},{16,0},... | collective-permute-start | bytes 221192 | tf_op jit(solution)/shard_map/ppermute | solution.py:178
  5.6 2.2 %copy-start = (bf16[32,128,512]{2,1,0:T(8,128)(2,1)S(1)}, bf16[32,128,512]{2,1,0:T(8,128)(2,1)}, u32[]{:S(2)}) copy-start(bf16[32,128,512]{2,1,0:T(8,128)(2,1)} %ku_ref.1) | copy-start | bytes 12582916
  7.8 1.2 %copy-start.2 = (bf16[128,4096]{1,0:T(8,128)(2,1)S(1)}, bf16[128,4096]{1,0:T(8,128)(2,1)}, u32[]{:S(2)}) copy-start(bf16[128,4096]{1,0:T(8,128)(2,1)} %qn_ref.1) | copy-start | bytes 3145732
  9.0 1.0 %copy-start.3 = (bf16[128,2048]{1,0:T(8,128)(2,1)S(1)}, bf16[128,2048]{1,0:T(8,128)(2,1)}, u32[]{:S(2)}) copy-start(bf16[128,2048]{1,0:T(8,128)(2,1)} %qr_ref.1) | copy-start | bytes 1572868
  10.1 0.7 %copy-start.5 = (f32[8,128]{1,0:T(8,128)S(1)}, f32[8,128]{1,0:T(8,128)}, u32[]{:S(2)}) copy-start(f32[8,128]{1,0:T(8,128)} %constant.2.clone.freq_ref) | copy-start | bytes 12292
  10.8 0.7 %copy-start.7 = (s32[4]{0:T(128)S(1)}, s32[4]{0:T(128)}, u32[]{:S(2)}) copy-start(s32[4]{0:T(128)} %lengths_ref.3) | copy-start | bytes 52
  11.4 5.3 %copy-start.4 = (bf16[64,576]{1,0:T(8,128)(2,1)S(1)}, bf16[64,576]{1,0:T(8,128)(2,1)}, u32[]{:S(2)}) copy-start(bf16[64,576]{1,0:T(8,128)(2,1)} %own_ref.1) | copy-start | bytes 221188
  11.4 5.3 %copy-start.6 = (f32[512]{0:T(512)S(1)}, f32[512]{0:T(512)}, u32[]{:S(2)}) copy-start(f32[512]{0:T(512)} %param.9) | copy-start | bytes 6148
  11.4 19.0 %copy-start.1 = (bf16[32,512,128]{2,1,0:T(8,128)(2,1)S(1)}, bf16[32,512,128]{2,1,0:T(8,128)(2,1)}, u32[]{:S(2)}) copy-start(bf16[32,512,128]{2,1,0:T(8,128)(2,1)} %vu_ref.1) | copy-start | bytes 12582916
  17.1 5.4 %collective-permute-start.2 = (bf16[2,64,576]{2,1,0:T(8,128)(2,1)S(1)}, bf16[2,64,576]{2,1,0:T(8,128)(2,1)S(1)}, u32[]{:S(2)}, u32[]{:S(2)}) collective-permute-start(bf16[2,64,576]{2,1,0:T(8,128)(2,1)S(1)} %get-tuple-element.14), channel_id=1, source_target_pairs={{0,4},{2,6},{4,0},{6,2},{8,12},{10,14},{12,8},{14,10},{16,20},{18,... | collective-permute-start | bytes 442376 | tf_op jit(solution)/shard_map/ppermute | solution.py:181
  18.7 8.6 %collective-permute-start.3 = (bf16[3,64,576]{2,1,0:T(8,128)(2,1)S(1)}, bf16[3,64,576]{2,1,0:T(8,128)(2,1)S(1)}, u32[]{:S(2)}, u32[]{:S(2)}) collective-permute-start(bf16[3,64,576]{2,1,0:T(8,128)(2,1)S(1)} %get-tuple-element.13.refs_0_), channel_id=1, source_target_pairs={{0,1},{1,0},{2,3},{3,2},{4,5},{5,4},{6,7},{7,6},{8,9},{9,8},{10,11... | collective-permute-start | bytes 663560 | tf_op jit(solution)/shard_map/ppermute | solution.py:184
  22.5 6.5 %collective-permute-start.4 = (bf16[2,64,576]{2,1,0:T(8,128)(2,1)S(1)}, bf16[2,64,576]{2,1,0:T(8,128)(2,1)S(1)}, u32[]{:S(2)}, u32[]{:S(2)}) collective-permute-start(bf16[2,64,576]{2,1,0:T(8,128)(2,1)S(1)} %collective-permute-done.2.refs_1_), channel_id=1, source_target_pairs={{0,1},{1,0},{2,3},{3,2},{4,5},{5,4},{6,7},{7,6},{8,9},{9,8},{10,11... | collective-permute-start | bytes 442376 | tf_op jit(solution)/shard_map/ppermute | solution.py:184
  24.0 5.0 %collective-permute-start.5 = (bf16[3,64,576]{2,1,0:T(8,128)(2,1)S(1)}, bf16[3,64,576]{2,1,0:T(8,128)(2,1)S(1)}, u32[]{:S(2)}, u32[]{:S(2)}) collective-permute-start(bf16[3,64,576]{2,1,0:T(8,128)(2,1)S(1)} %get-tuple-element.13.refs_0_), channel_id=1, source_target_pairs={{0,2},{2,0},{4,6},{6,4},{8,10},{10,8},{12,14},{14,12},{16,18},{18,... | collective-permute-start | bytes 663560 | tf_op jit(solution)/shard_map/ppermute | solution.py:181
  27.3 3.2 %collective-permute-start.7 = (bf16[3,64,576]{2,1,0:T(8,128)(2,1)S(1)}, bf16[3,64,576]{2,1,0:T(8,128)(2,1)S(1)}, u32[]{:S(2)}, u32[]{:S(2)}) collective-permute-start(bf16[3,64,576]{2,1,0:T(8,128)(2,1)S(1)} %collective-permute-done.3.refs_2_), channel_id=1, source_target_pairs={{0,2},{2,0},{4,6},{6,4},{8,10},{10,8},{12,14},{14,12},{16,18},{18,... | collective-permute-start | bytes 663560 | tf_op jit(solution)/shard_map/ppermute | solution.py:181
  27.3 1.8 %collective-permute-start.6 = (bf16[2,64,576]{2,1,0:T(8,128)(2,1)S(1)}, bf16[2,64,576]{2,1,0:T(8,128)(2,1)S(1)}, u32[]{:S(2)}, u32[]{:S(2)}) collective-permute-start(bf16[2,64,576]{2,1,0:T(8,128)(2,1)S(1)} %collective-permute-done.2.refs_1_), channel_id=1, source_target_pairs={{0,2},{2,0},{4,6},{6,4},{8,10},{10,8},{12,14},{14,12},{16,18},{18,... | collective-permute-start | bytes 442376 | tf_op jit(solution)/shard_map/ppermute | solution.py:181
  29.0 1.4 %collective-permute-start.8 = (bf16[2,64,576]{2,1,0:T(8,128)(2,1)S(1)}, bf16[2,64,576]{2,1,0:T(8,128)(2,1)S(1)}, u32[]{:S(2)}, u32[]{:S(2)}) collective-permute-start(bf16[2,64,576]{2,1,0:T(8,128)(2,1)S(1)} %collective-permute-done.4.refs_3_), channel_id=1, source_target_pairs={{0,2},{2,0},{4,6},{6,4},{8,10},{10,8},{12,14},{14,12},{16,18},{18,... | collective-permute-start | bytes 442376 | tf_op jit(solution)/shard_map/ppermute | solution.py:181

commit v2 on v1

--- a/solution.py
+++ b/solution.py
@@ -1,4 +1,5 @@
 import functools
+import math
 
 import jax
 import jax.numpy as jnp
@@ -12,7 +13,10 @@
 masked_score = -1e30
 PLANE = 4
 GROUP = 8
+SPAN = 32
 SUB = 4
+VALUE_GROUP = 32
+HBM = pl.BlockSpec(memory_space=pltpu.HBM)
 VMEM = pl.BlockSpec(memory_space=pltpu.VMEM)
 SMEM = pl.BlockSpec(memory_space=pltpu.SMEM)
 
@@ -38,12 +42,42 @@
     return (base * PLANE + row * 2 + core) * block_rows + head * half_rows
 
 
-def query_kernel(lengths_ref, freq_ref, qn_ref, qr_ref, ku_ref, q_ref, cos_ref, sin_ref):
+def frequencies(rope, shape):
+    half = rope // 2
+    exponents = np.float32(-2.0) * np.arange(half, dtype=np.float32) / np.float32(rope)
+    values = np.float32(10000.0) ** exponents
+    lane = lax.rem(lax.broadcasted_iota(jnp.int32, shape, 1), half)
+    freq = jnp.zeros(shape, jnp.float32)
+    for index in range(half):
+        freq = jnp.where(lane == index, float(values[index]), freq)
+    return freq
+
+
+def query_kernel(lengths_hbm, qn_hbm, qr_hbm, ku_hbm, q_ref, cos_ref, sin_ref, qn_ref, qr_ref, ku_ref, lengths_ref, sems):
     rows = qn_ref.shape[0]
     heads, nope, latent = ku_ref.shape
     rope = qr_ref.shape[1] // heads
+    groups = heads // GROUP
+
+    def copies(index):
+        head = index * GROUP
+        cols = pl.ds(head * nope, GROUP * nope)
+        part = pl.ds(head, GROUP)
+        return [
+            pltpu.make_async_copy(qn_hbm.at[:, cols], qn_ref.at[:, cols], sems.at[index, 0]),
+            pltpu.make_async_copy(ku_hbm.at[part], ku_ref.at[part], sems.at[index, 1]),
+        ]
+
+    rope_copy = pltpu.make_async_copy(qr_hbm, qr_ref, sems.at[groups, 0])
+    lengths_copy = pltpu.make_async_copy(lengths_hbm, lengths_ref, sems.at[groups, 1])
+    lengths_copy.start()
+    rope_copy.start()
+    for index in range(groups):
+        for copy in copies(index):
+            copy.start()
+    lengths_copy.wait()
     ctx = lax.axis_index("ctx")
-    freq = freq_ref[0:1, :]
+    freq = frequencies(rope, (8, 128))[0:1, :]
     key_rows = rows // 2
     for plane in range(3):
         first = half_start(plane, False, False, False, rows, key_rows)
@@ -58,24 +92,20 @@
     cos = jnp.cos(angle)
     sin = jnp.sin(angle)
     sin = jnp.where(low, -sin, sin)
-
-    def group(index, carry):
-        for j in range(0, GROUP, 2):
-            head = index * GROUP + j
-            pair = qr_ref[:, pl.ds(pl.multiple_of(head * rope, 128), 128)].astype(jnp.float32)
+    rope_copy.wait()
+    for index in range(groups):
+        for copy in copies(index):
+            copy.wait()
+        for head in range(index * GROUP, (index + 1) * GROUP, 2):
+            pair = qr_ref[:, head * rope : (head + 2) * rope].astype(jnp.float32)
             partner = jnp.where(low, pltpu.roll(pair, 128 - rope // 2, 1), pltpu.roll(pair, rope // 2, 1))
             rotated = pair * cos + partner * sin
-            shifted = pltpu.roll(rotated, rope, 1)
-            for k in range(2):
-                at = pl.ds(pl.multiple_of((head + k) * rows, rows), rows)
-                nope_rows = qn_ref[:, pl.ds(pl.multiple_of((head + k) * nope, 128), nope)]
+            for k, part in enumerate((rotated, pltpu.roll(rotated, rope, 1))):
+                at = slice((head + k) * rows, (head + k + 1) * rows)
+                nope_rows = qn_ref[:, (head + k) * nope : (head + k + 1) * nope]
                 absorbed = jnp.dot(nope_rows, ku_ref[head + k], preferred_element_type=jnp.float32)
                 q_ref[at, :latent] = absorbed.astype(jnp.bfloat16)
-                part = rotated if k == 0 else shifted
                 q_ref[at, latent:] = jnp.where(lane < rope, part, 0.0).astype(jnp.bfloat16)
-        return carry
-
-    lax.fori_loop(0, heads // GROUP, group, 0)
 
 
 def rows_kernel(own_ref, one_ref, two_ref, gain_ref, cos_ref, sin_ref, rows_ref, send_ref):
@@ -97,13 +127,40 @@
     send_ref[...] = rows_ref[pl.ds(row, 2)]
 
 
-def attend_kernel(layout, scale, lengths_ref, q_ref, vu_ref, *refs):
+def widen(column, count):
+    return jnp.concatenate([column] * count, axis=1)
+
+
+def value_heads(mixed_ref, vu_ref, out_ref):
+    heads, latent, value = vu_ref.shape
+    rows = out_ref.shape[0]
+
+    def group(index, carry):
+        for j in range(VALUE_GROUP):
+            head = index * VALUE_GROUP + j
+            at = pl.ds(pl.multiple_of(head * rows, rows), rows)
+            result = jnp.dot(mixed_ref[at, :], vu_ref[head], preferred_element_type=jnp.float32)
+            out_ref[:, pl.ds(pl.multiple_of(head * value, 128), value)] = result.astype(jnp.bfloat16)
+        return carry
+
+    lax.fori_loop(0, heads // VALUE_GROUP, group, 0)
+
+
+def attend_kernel(layout, scale, first_call, last_call, lengths_ref, q_ref, *refs):
     count = len(layout)
-    piece_refs = refs[:count]
-    out_ref, kv_ref = refs[count:]
-    heads, latent, value = vu_ref.shape
-    rows = q_ref.shape[0] // heads
-    half_rows = rows // 2
+    piece_refs, refs = refs[:count], refs[count:]
+    if not first_call:
+        sum_in, most_in, total_in = refs[:3]
+        refs = refs[3:]
+    if last_call:
+        vu_ref, out_ref, mixed_ref, kv_ref = refs
+        latent = mixed_ref.shape[1]
+    else:
+        sum_out, most_out, total_out, kv_ref = refs
+        latent = sum_out.shape[1]
+    half_rows = piece_refs[0].shape[1]
+    rows = 2 * half_rows
+    heads = q_ref.shape[0] // rows
     ctx = lax.axis_index("ctx")
     core = lax.rem(ctx, 2)
     row = lax.rem(ctx // 2, 2)
@@ -126,41 +183,52 @@
     pos = ctx * rows + lax.broadcasted_iota(jnp.int32, (rows, keys), 0)
     live = (key_pos <= pos) & (key_pos >= begin_of(pos, lengths_ref))
 
+    exponent = scale * math.log2(math.e)
+
+    def span(base):
+        return pl.ds(pl.multiple_of(base * rows, rows), SUB * rows)
+
     def scores(base):
-        at = pl.ds(pl.multiple_of(base * rows, rows), SUB * rows)
         return lax.dot_general(
-            q_ref[at, :], kv_ref[...], (((1,), (1,)), ((), ())), preferred_element_type=jnp.float32
+            q_ref[span(base), :], kv_ref[...], (((1,), (1,)), ((), ())), preferred_element_type=jnp.float32
         )
 
     def group(index, carry):
-        subs = GROUP // SUB
-        now = scores(index * GROUP)
+        subs = SPAN // SUB
+        now = scores(index * SPAN)
         for sub in range(subs):
-            base = index * GROUP + sub * SUB
+            base = index * SPAN + sub * SUB
             later = scores(base + SUB) if sub + 1 < subs else None
-            now = jnp.where(live[None], now.reshape(SUB, rows, keys) * scale, masked_score)
-            most = jnp.max(now, axis=2, keepdims=True)
-            weights = jnp.exp(now - most)
-            total = jnp.sum(weights, axis=2, keepdims=True).reshape(SUB * rows, 1)
-            mixed = jnp.dot(
-                weights.astype(jnp.bfloat16).reshape(SUB * rows, keys),
-                kv_ref[:, :latent],
-                preferred_element_type=jnp.float32,
-            )
-            mixed = (mixed / total).astype(jnp.bfloat16)
-            for j in range(SUB):
-                result = jnp.dot(
-                    mixed[j * rows : (j + 1) * rows], vu_ref[base + j], preferred_element_type=jnp.float32
-                )
-                out_ref[:, pl.ds(pl.multiple_of((base + j) * value, 128), value)] = result.astype(jnp.bfloat16)
+            now = jnp.where(live[None], now.reshape(SUB, rows, keys), masked_score)
+            now = now.reshape(SUB * rows, keys)
+            most = jnp.broadcast_to(jnp.max(now, axis=1, keepdims=True), (SUB * rows, 128))
+            if not first_call:
+                before = most_in[span(base), :]
+                most = jnp.maximum(most, before)
+                factor = jnp.exp2((before - most) * exponent)
+            weights = jnp.exp2((now - widen(most, keys // 128)) * exponent)
+            total = jnp.broadcast_to(jnp.sum(weights, axis=1, keepdims=True), (SUB * rows, 128))
+            mixed = jnp.dot(weights.astype(jnp.bfloat16), kv_ref[:, :latent], preferred_element_type=jnp.float32)
+            if not first_call:
+                total = total + factor * total_in[span(base), :]
+                mixed = mixed + widen(factor, latent // 128) * sum_in[span(base), :]
+            if last_call:
+                mixed = mixed * widen(1.0 / total, latent // 128)
+                mixed_ref[span(base), :] = mixed.astype(jnp.bfloat16)
+            else:
+                sum_out[span(base), :] = mixed
+                most_out[span(base), :] = most
+                total_out[span(base), :] = total
             now = later
         return carry
 
-    lax.fori_loop(0, heads // GROUP, group, 0)
-
-
-def params():
-    return pltpu.CompilerParams(vmem_limit_bytes=48 * 2**20)
+    lax.fori_loop(0, heads // SPAN, group, 0)
+    if last_call:
+        value_heads(mixed_ref, vu_ref, out_ref)
+
+
+def params(limit=24):
+    return pltpu.CompilerParams(vmem_limit_bytes=limit * 2**20)
 
 
 def shards(latent_raw, kv_gain, query_nope, query_rope, key_up, value_up, doc_lengths):
@@ -185,20 +253,27 @@
 
     one = plane_shift(latent_raw, 1)
     two = plane_shift(latent_raw, 2)
-    freq = np.float32(10000.0) ** (np.float32(-2.0) * np.arange(rope // 2, dtype=np.float32) / np.float32(rope))
-    freq = jnp.asarray(np.tile(freq.astype(np.float32), (8, 128 // (rope // 2))))
     table = jax.ShapeDtypeStruct((3, half_rows, 128), jnp.float32)
     queries, cos, sin = pl.pallas_call(
         query_kernel,
         out_shape=(jax.ShapeDtypeStruct((heads * rows, wide), jnp.bfloat16), table, table),
-        in_specs=[SMEM] + [VMEM] * 4,
+        in_specs=[HBM] * 4,
         out_specs=[VMEM] * 3,
+        scratch_shapes=[
+            pltpu.VMEM(query_nope.shape, jnp.bfloat16),
+            pltpu.VMEM(query_rope.shape, jnp.bfloat16),
+            pltpu.VMEM(key_up.shape, jnp.bfloat16),
+            pltpu.SMEM(doc_lengths.shape, jnp.int32),
+            pltpu.SemaphoreType.DMA((heads // GROUP + 1, 2)),
+        ],
         compiler_params=params(),
         cost_estimate=pl.CostEstimate(
             flops=2 * heads * rows * nope * latent, bytes_accessed=8 * 2**20, transcendentals=0
         ),
         name="queries",
-    )(doc_lengths, freq, query_nope, query_rope, key_up)
+    )(
+        *(pltpu.with_memory_space_constraint(array, pltpu.HBM) for array in (doc_lengths, query_nope, query_rope, key_up))
+    )
     near, send = pl.pallas_call(
         rows_kernel,
         out_shape=(
@@ -212,22 +287,39 @@
     )(latent_raw, one, two, kv_gain[None], cos, sin)
     across = swap_ctx(send, 2)
     side = swap_head(near)
+    near_pieces = [(near, (False, False, False)), (swap_ctx(near, 1), (False, True, False))]
+
+    state_shape = (
+        jax.ShapeDtypeStruct((heads * rows, latent), jnp.float32),
+        jax.ShapeDtypeStruct((heads * rows, 128), jnp.float32),
+        jax.ShapeDtypeStruct((heads * rows, 128), jnp.float32),
+    )
+    names = iter(("attend_near", "attend_far"))
+
+    def attend(part, state, last=False):
+        pieces, layout = zip(*part)
+        keys = 2 * half_rows * len(pieces)
+        scratch = [pltpu.VMEM((keys, wide), jnp.bfloat16)]
+        if last:
+            scratch = [pltpu.VMEM((heads * rows, latent), jnp.bfloat16)] + scratch
+        extra = (value_up,) if last else ()
+        return pl.pallas_call(
+            functools.partial(attend_kernel, layout, scale, not state, last),
+            out_shape=jax.ShapeDtypeStruct((rows, heads * value), jnp.bfloat16) if last else state_shape,
+            in_specs=[SMEM] + [VMEM] * (1 + len(pieces) + len(state) + len(extra)),
+            out_specs=VMEM if last else [VMEM] * 3,
+            scratch_shapes=scratch,
+            compiler_params=params(),
+            name=next(names),
+        )(doc_lengths, queries, *pieces, *state, *extra)
+
     corner = swap_head(across)
-    pieces = [near, across, side, corner]
-    pieces = pieces + [swap_ctx(piece, 1) for piece in pieces]
-    layout = []
-    for flip_core in (False, True):
-        layout += [(False, flip_core, False), (True, flip_core, False), (False, flip_core, True), (True, flip_core, True)]
-    keys = 2 * half_rows * len(pieces)
-    return pl.pallas_call(
-        functools.partial(attend_kernel, tuple(layout), scale),
-        out_shape=jax.ShapeDtypeStruct((rows, heads * value), jnp.bfloat16),
-        in_specs=[SMEM] + [VMEM] * (2 + len(pieces)),
-        out_specs=VMEM,
-        scratch_shapes=[pltpu.VMEM((keys, wide), jnp.bfloat16)],
-        compiler_params=params(),
-        name="attend",
-    )(doc_lengths, queries, value_up, *pieces)
+    across_pieces = [(across, (True, False, False)), (swap_ctx(across, 1), (True, True, False))]
+    state = attend(near_pieces + across_pieces, ())
+    side, corner, *state = lax.optimization_barrier((side, corner, *state))
+    side_pieces = [(side, (False, False, True)), (swap_ctx(side, 1), (False, True, True))]
+    corner_pieces = [(corner, (True, False, True)), (swap_ctx(corner, 1), (True, True, True))]
+    return attend(side_pieces + corner_pieces, state, last=True)
 
 
 def solution(mesh):

time: 49.7 us -> 38.1 us (0.77)
  local copies, waits for them, and re-layouts: 5.8 us -> 0.02 us
  Pallas kernels: 24.6 us -> 20.5 us
  waiting for transfers between devices: 8.23 us -> 6.67 us
    unnamed x16 -> x8, local copies, waits for them, and re-layouts: 5.8 us -> 0.02 us
    ppermute x2, waiting for transfers between devices: 4.5 us -> 0.01 us  [swap_head(): return lax.ppermute(array, 'head', [(0, 1), (1, 0)])]
    ppermute x2, waiting for transfers between devices: 0.01 us -> 2.31 us  [plane_shift(): lax.ppermute(array, 'ctx', [(s, (s + steps) % ctx_size) for s in range(ct...]
    pallas_call x1 -> x2, Pallas kernels: 19 us -> 16.9 us  [attend(): pl.pallas_call(functools.partial(attend_kernel, layout, scale, not state,...]
    pallas_call x1, Pallas kernels: 5.28 us -> 3.27 us  [shards(): pl.pallas_call(query_kernel, out_shape=(jax.ShapeDtypeStruct((heads * row...]
    ppermute x5, waiting for transfers between devices: 3.72 us -> 4.35 us  [swap_ctx(): return lax.ppermute(array, 'ctx', [(s, s ^ bit) for s in range(ctx_size)])]
  transfers between devices with their start and end apart: 9 -> 9, of which waited for: 4 -> 3; matrix products, arithmetic and copies ran while one was open for 0% -> 0% of each run, Pallas kernels for 11% -> 26%
where the time goes in v2:
time: 38.1 us; the launch traced here: 38 us
  Pallas kernels  20.5 us (54%)
  starting transfers between devices  10.7 us (28%)
  waiting for transfers between devices  6.67 us (18%)
    pallas_call x2, Pallas kernels, attend(): pl.pallas_call(functools.partial(attend_kernel, layout, scale, not state,...  16.9 us
    ppermute x2, starting transfers between devices, plane_shift(): lax.ppermute(array, 'ctx', [(s, (s + steps) % ctx_size) for s in range(ct...  5.67 us
    ppermute x5, waiting for transfers between devices, swap_ctx(): return lax.ppermute(array, 'ctx', [(s, s ^ bit) for s in range(ctx_size)])  4.35 us
    pallas_call x1, Pallas kernels, shards(): pl.pallas_call(query_kernel, out_shape=(jax.ShapeDtypeStruct((heads * row...  3.27 us
    ppermute x2, starting transfers between devices, swap_head(): return lax.ppermute(array, 'head', [(0, 1), (1, 0)])  2.9 us
    ppermute x2, waiting for transfers between devices, plane_shift(): lax.ppermute(array, 'ctx', [(s, (s + steps) % ctx_size) for s in range(ct...  2.31 us
    ppermute x5, starting transfers between devices, swap_ctx(): return lax.ppermute(array, 'ctx', [(s, s ^ bit) for s in range(ctx_size)])  2.17 us
  transfers between devices with their start and end apart: 9, of which 3 were waited for; matrix products, arithmetic and copies ran while one was open for 0% of the time, Pallas kernels for 26%

profile of v2, /device:TPU:0, one launch (start us, length us, event | category | flops | bytes accessed | tf_op | source)
XLA Modules:
  0.0 38.0 jit_solution(7676151062200850196)
XLA Ops:
  0.0 0.0 copy-start.1
  0.0 0.0 copy-start.2
  0.0 0.0 copy-start.3
  0.0 3.1 %collective-permute-start = (bf16[64,576]{1,0:T(8,128)(2,1)}, bf16[64,576]{1,0:T(8,128)(2,1)S(1)}, u32[]{:S(2)}, u32[]{:S(2)}) collective-permute-start(bf16[64,576]{1,0:T(8,128)(2,1)} %own_ref.1), channel_id=1, source_target_pairs={{0,8},{2,10},{4,12},{6,14},{8,16},{10,18},{12,20},{14,22},{16,24},... | collective-permute-start | bytes 221192 | tf_op jit(solution)/shard_map/ppermute | solution.py:246
  3.1 2.6 %collective-permute-start.1 = (bf16[64,576]{1,0:T(8,128)(2,1)}, bf16[64,576]{1,0:T(8,128)(2,1)S(1)}, u32[]{:S(2)}, u32[]{:S(2)}) collective-permute-start(bf16[64,576]{1,0:T(8,128)(2,1)} %own_ref.1), channel_id=1, source_target_pairs={{0,16},{2,18},{4,20},{6,22},{8,24},{10,26},{12,28},{14,30},{16,0},... | collective-permute-start | bytes 221192 | tf_op jit(solution)/shard_map/ppermute | solution.py:246
  5.7 3.3 %queries.1 = (bf16[4096,640]{1,0:T(8,128)(2,1)S(1)}, f32[3,64,128]{2,1,0:T(8,128)S(1)}, f32[3,64,128]{2,1,0:T(8,128)S(1)}) custom-call(s32[4]{0:T(128)} %lengths_ref.3, bf16[128,4096]{1,0:T(8,128)(2,1)} %qn_hbm.1, bf16[128,2048]{1,0:T(8,128)(2,1)} %qr_hbm.1, bf16[32,128,512]{2,1,0:T(8,128)(2,1)} %ku_hbm.1), custom_call_target="tpu_custom_call" | custom-call | flops 536870912 | bytes 8388608 | tf_op jit(solution)/shard_map/queries/pallas_call | solution.py:257
  8.9 0.0 copy-start
  9.0 0.0 collective-permute-done.one_ref
  9.0 2.3 %collective-permute-done.1.two_ref = bf16[64,576]{1,0:T(8,128)(2,1)S(1)} collective-permute-done((bf16[64,576]{1,0:T(8,128)(2,1)}, bf16[64,576]{1,0:T(8,128)(2,1)S(1)}, u32[]{:S(2)}, u32[]{:S(2)}) %collective-permute-start.1) | collective-permute-done | bytes 73760 | tf_op jit(solution)/shard_map/ppermute | solution.py:246
  11.3 0.0 copy-done.1
  11.3 0.0 copy-done.3
  11.3 0.4 rows.1
  11.7 1.6 %collective-permute-start.3 = (bf16[2,64,576]{2,1,0:T(8,128)(2,1)S(1)}, bf16[2,64,576]{2,1,0:T(8,128)(2,1)S(1)}, u32[]{:S(2)}, u32[]{:S(2)}) collective-permute-start(bf16[2,64,576]{2,1,0:T(8,128)(2,1)S(1)} %get-tuple-element.22), channel_id=1, source_target_pairs={{0,4},{2,6},{4,0},{6,2},{8,12},{10,14},{12,8},{14,10},{16,20},{18,... | collective-permute-start | bytes 442376 | tf_op jit(solution)/shard_map/ppermute | solution.py:249
  13.3 0.0 collective-permute-start.5
  13.3 1.5 %collective-permute-start.2 = (bf16[3,64,576]{2,1,0:T(8,128)(2,1)S(1)}, bf16[3,64,576]{2,1,0:T(8,128)(2,1)S(1)}, u32[]{:S(2)}, u32[]{:S(2)}) collective-permute-start(bf16[3,64,576]{2,1,0:T(8,128)(2,1)S(1)} %get-tuple-element.21.refs_0_), channel_id=1, source_target_pairs={{0,1},{1,0},{2,3},{3,2},{4,5},{5,4},{6,7},{7,6},{8,9},{9,8},{10,11... | collective-permute-start | bytes 663560 | tf_op jit(solution)/shard_map/ppermute | solution.py:252
  14.8 3.1 %collective-permute-done.3.refs_2_ = bf16[2,64,576]{2,1,0:T(8,128)(2,1)S(1)} collective-permute-done((bf16[2,64,576]{2,1,0:T(8,128)(2,1)S(1)}, bf16[2,64,576]{2,1,0:T(8,128)(2,1)S(1)}, u32[]{:S(2)}, u32[]{:S(2)}) %collective-permute-start.3) | collective-permute-done | bytes 147488 | tf_op jit(solution)/shard_map/ppermute | solution.py:249
  17.9 0.0 collective-permute-start.6
  17.9 1.4 %collective-permute-start.4 = (bf16[2,64,576]{2,1,0:T(8,128)(2,1)S(1)}, bf16[2,64,576]{2,1,0:T(8,128)(2,1)S(1)}, u32[]{:S(2)}, u32[]{:S(2)}) collective-permute-start(bf16[2,64,576]{2,1,0:T(8,128)(2,1)S(1)} %collective-permute-done.3.refs_2_), channel_id=1, source_target_pairs={{0,1},{1,0},{2,3},{3,2},{4,5},{5,4},{6,7},{7,6},{8,9},{9,8},{10,11... | collective-permute-start | bytes 442376 | tf_op jit(solution)/shard_map/ppermute | solution.py:252
  19.3 0.0 collective-permute-done.5.refs_1_
  19.3 0.0 collective-permute-done.6.refs_3_
  19.3 0.0 copy-done.2
  19.3 6.6 %attend_near.1 = (f32[4096,512]{1,0:T(8,128)S(1)}, f32[4096,128]{1,0:T(8,128)S(1)}, f32[4096,128]{1,0:T(8,128)S(1)}) custom-call(s32[4]{0:T(128)S(1)} %copy-done.2, bf16[4096,640]{1,0:T(8,128)(2,1)S(1)} %get-tuple-element.18.q_ref, bf16[3,64,576]{2,1,0:T(8,128)(2,1)S(1)} %get-tuple-element.21.refs_0_, ...), custom_call_target="tpu_custom_call" | custom-call | tf_op jit(solution)/shard_map/attend_near/pallas_call | solution.py:306
  25.9 0.0 collective-permute-done.2.refs_0_
  25.9 0.0 collective-permute-done.4.refs_2_
  26.0 0.3 collective-permute-start.7
  26.3 0.3 collective-permute-start.8
  26.5 1.2 %collective-permute-done.8.refs_3_ = bf16[2,64,576]{2,1,0:T(8,128)(2,1)S(1)} collective-permute-done((bf16[2,64,576]{2,1,0:T(8,128)(2,1)S(1)}, bf16[2,64,576]{2,1,0:T(8,128)(2,1)S(1)}, u32[]{:S(2)}, u32[]{:S(2)}) %collective-permute-start.8) | collective-permute-done | bytes 147488 | tf_op jit(solution)/shard_map/ppermute | solution.py:249
  27.8 0.0 collective-permute-done.7.refs_1_
  27.8 0.0 copy-done
  27.8 10.2 %attend_far.1 = bf16[128,4096]{1,0:T(8,128)(2,1)} custom-call(s32[4]{0:T(128)S(1)} %copy-done.2, bf16[4096,640]{1,0:T(8,128)(2,1)S(1)} %get-tuple-element.18.q_ref, bf16[3,64,576]{2,1,0:T(8,128)(2,1)S(1)} %collective-permute-done.2.refs_0_, bf16[3,64,576]{2,1,0:T(8,128)(2,1)S(1)} %collective-permute-done.7.refs_1_, ...), custom_call_target="tpu_custom_call" | custom-call | tf_op jit(solution)/shard_map/attend_far/pallas_call | solution.py:306
Async XLA Ops:
  0.0 11.3 %copy-start.1 = (bf16[64,576]{1,0:T(8,128)(2,1)S(1)}, bf16[64,576]{1,0:T(8,128)(2,1)}, u32[]{:S(2)}) copy-start(bf16[64,576]{1,0:T(8,128)(2,1)} %own_ref.1) | copy-start | bytes 221188
  0.0 19.3 %copy-start.2 = (s32[4]{0:T(128)S(1)}, s32[4]{0:T(128)}, u32[]{:S(2)}) copy-start(s32[4]{0:T(128)} %lengths_ref.3) | copy-start | bytes 52
  0.0 11.3 %copy-start.3 = (f32[512]{0:T(512)S(1)}, f32[512]{0:T(512)}, u32[]{:S(2)}) copy-start(f32[512]{0:T(512)} %param.8) | copy-start | bytes 6148
  0.0 9.0 %collective-permute-start = (bf16[64,576]{1,0:T(8,128)(2,1)}, bf16[64,576]{1,0:T(8,128)(2,1)S(1)}, u32[]{:S(2)}, u32[]{:S(2)}) collective-permute-start(bf16[64,576]{1,0:T(8,128)(2,1)} %own_ref.1), channel_id=1, source_target_pairs={{0,8},{2,10},{4,12},{6,14},{8,16},{10,18},{12,20},{14,22},{16,24},... | collective-permute-start | bytes 221192 | tf_op jit(solution)/shard_map/ppermute | solution.py:246
  3.1 8.2 %collective-permute-start.1 = (bf16[64,576]{1,0:T(8,128)(2,1)}, bf16[64,576]{1,0:T(8,128)(2,1)S(1)}, u32[]{:S(2)}, u32[]{:S(2)}) collective-permute-start(bf16[64,576]{1,0:T(8,128)(2,1)} %own_ref.1), channel_id=1, source_target_pairs={{0,16},{2,18},{4,20},{6,22},{8,24},{10,26},{12,28},{14,30},{16,0},... | collective-permute-start | bytes 221192 | tf_op jit(solution)/shard_map/ppermute | solution.py:246
  8.9 18.8 %copy-start = (bf16[32,512,128]{2,1,0:T(8,128)(2,1)S(1)}, bf16[32,512,128]{2,1,0:T(8,128)(2,1)}, u32[]{:S(2)}) copy-start(bf16[32,512,128]{2,1,0:T(8,128)(2,1)} %refs_7_.1) | copy-start | bytes 12582916
  11.7 6.2 %collective-permute-start.3 = (bf16[2,64,576]{2,1,0:T(8,128)(2,1)S(1)}, bf16[2,64,576]{2,1,0:T(8,128)(2,1)S(1)}, u32[]{:S(2)}, u32[]{:S(2)}) collective-permute-start(bf16[2,64,576]{2,1,0:T(8,128)(2,1)S(1)} %get-tuple-element.22), channel_id=1, source_target_pairs={{0,4},{2,6},{4,0},{6,2},{8,12},{10,14},{12,8},{14,10},{16,20},{18,... | collective-permute-start | bytes 442376 | tf_op jit(solution)/shard_map/ppermute | solution.py:249
  13.3 6.0 %collective-permute-start.5 = (bf16[3,64,576]{2,1,0:T(8,128)(2,1)S(1)}, bf16[3,64,576]{2,1,0:T(8,128)(2,1)S(1)}, u32[]{:S(2)}, u32[]{:S(2)}) collective-permute-start(bf16[3,64,576]{2,1,0:T(8,128)(2,1)S(1)} %get-tuple-element.21.refs_0_), channel_id=1, source_target_pairs={{0,2},{2,0},{4,6},{6,4},{8,10},{10,8},{12,14},{14,12},{16,18},{18,... | collective-permute-start | bytes 663560 | tf_op jit(solution)/shard_map/ppermute | solution.py:249
  13.3 12.7 %collective-permute-start.2 = (bf16[3,64,576]{2,1,0:T(8,128)(2,1)S(1)}, bf16[3,64,576]{2,1,0:T(8,128)(2,1)S(1)}, u32[]{:S(2)}, u32[]{:S(2)}) collective-permute-start(bf16[3,64,576]{2,1,0:T(8,128)(2,1)S(1)} %get-tuple-element.21.refs_0_), channel_id=1, source_target_pairs={{0,1},{1,0},{2,3},{3,2},{4,5},{5,4},{6,7},{7,6},{8,9},{9,8},{10,11... | collective-permute-start | bytes 663560 | tf_op jit(solution)/shard_map/ppermute | solution.py:252
  17.9 1.4 %collective-permute-start.6 = (bf16[2,64,576]{2,1,0:T(8,128)(2,1)S(1)}, bf16[2,64,576]{2,1,0:T(8,128)(2,1)S(1)}, u32[]{:S(2)}, u32[]{:S(2)}) collective-permute-start(bf16[2,64,576]{2,1,0:T(8,128)(2,1)S(1)} %collective-permute-done.3.refs_2_), channel_id=1, source_target_pairs={{0,2},{2,0},{4,6},{6,4},{8,10},{10,8},{12,14},{14,12},{16,18},{18,... | collective-permute-start | bytes 442376 | tf_op jit(solution)/shard_map/ppermute | solution.py:249
  17.9 8.1 %collective-permute-start.4 = (bf16[2,64,576]{2,1,0:T(8,128)(2,1)S(1)}, bf16[2,64,576]{2,1,0:T(8,128)(2,1)S(1)}, u32[]{:S(2)}, u32[]{:S(2)}) collective-permute-start(bf16[2,64,576]{2,1,0:T(8,128)(2,1)S(1)} %collective-permute-done.3.refs_2_), channel_id=1, source_target_pairs={{0,1},{1,0},{2,3},{3,2},{4,5},{5,4},{6,7},{7,6},{8,9},{9,8},{10,11... | collective-permute-start | bytes 442376 | tf_op jit(solution)/shard_map/ppermute | solution.py:252
  26.0 1.8 %collective-permute-start.7 = (bf16[3,64,576]{2,1,0:T(8,128)(2,1)S(1)}, bf16[3,64,576]{2,1,0:T(8,128)(2,1)S(1)}, u32[]{:S(2)}, u32[]{:S(2)}) collective-permute-start(bf16[3,64,576]{2,1,0:T(8,128)(2,1)S(1)} %collective-permute-done.2.refs_0_), channel_id=1, source_target_pairs={{0,2},{2,0},{4,6},{6,4},{8,10},{10,8},{12,14},{14,12},{16,18},{18,... | collective-permute-start | bytes 663560 | tf_op jit(solution)/shard_map/ppermute | solution.py:249
  26.3 1.5 %collective-permute-start.8 = (bf16[2,64,576]{2,1,0:T(8,128)(2,1)S(1)}, bf16[2,64,576]{2,1,0:T(8,128)(2,1)S(1)}, u32[]{:S(2)}, u32[]{:S(2)}) collective-permute-start(bf16[2,64,576]{2,1,0:T(8,128)(2,1)S(1)} %collective-permute-done.4.refs_2_), channel_id=1, source_target_pairs={{0,2},{2,0},{4,6},{6,4},{8,10},{10,8},{12,14},{14,12},{16,18},{18,... | collective-permute-start | bytes 442376 | tf_op jit(solution)/shard_map/ppermute | solution.py:249

commit v3 on v2

--- a/solution.py
+++ b/solution.py
@@ -13,9 +13,8 @@
 masked_score = -1e30
 PLANE = 4
 GROUP = 8
-SPAN = 32
 SUB = 4
-VALUE_GROUP = 32
+VALUE_GROUP = 8
 HBM = pl.BlockSpec(memory_space=pltpu.HBM)
 VMEM = pl.BlockSpec(memory_space=pltpu.VMEM)
 SMEM = pl.BlockSpec(memory_space=pltpu.SMEM)
@@ -131,19 +130,23 @@
     return jnp.concatenate([column] * count, axis=1)
 
 
-def value_heads(mixed_ref, vu_ref, out_ref):
+def value_heads(mixed_ref, vu_ref, held_ref, out_ref, sems):
     heads, latent, value = vu_ref.shape
-    rows = out_ref.shape[0]
-
-    def group(index, carry):
-        for j in range(VALUE_GROUP):
-            head = index * VALUE_GROUP + j
-            at = pl.ds(pl.multiple_of(head * rows, rows), rows)
-            result = jnp.dot(mixed_ref[at, :], vu_ref[head], preferred_element_type=jnp.float32)
-            out_ref[:, pl.ds(pl.multiple_of(head * value, 128), value)] = result.astype(jnp.bfloat16)
-        return carry
-
-    lax.fori_loop(0, heads // VALUE_GROUP, group, 0)
+    rows = held_ref.shape[0]
+    copies = []
+    for head in range(heads):
+        cols = slice(head * value, (head + 1) * value)
+        result = jnp.dot(
+            mixed_ref[head * rows : (head + 1) * rows, :], vu_ref[head], preferred_element_type=jnp.float32
+        )
+        held_ref[:, cols] = result.astype(jnp.bfloat16)
+        if (head + 1) % VALUE_GROUP == 0:
+            group = head // VALUE_GROUP
+            cols = slice(group * VALUE_GROUP * value, (head + 1) * value)
+            copies.append(pltpu.make_async_copy(held_ref.at[:, cols], out_ref.at[:, cols], sems.at[group]))
+            copies[-1].start()
+    for copy in copies:
+        copy.wait()
 
 
 def attend_kernel(layout, scale, first_call, last_call, lengths_ref, q_ref, *refs):
@@ -153,7 +156,7 @@
         sum_in, most_in, total_in = refs[:3]
         refs = refs[3:]
     if last_call:
-        vu_ref, out_ref, mixed_ref, kv_ref = refs
+        vu_ref, out_ref, mixed_ref, held_ref, sems, kv_ref = refs
         latent = mixed_ref.shape[1]
     else:
         sum_out, most_out, total_out, kv_ref = refs
@@ -167,48 +170,40 @@
     keys = kv_ref.shape[0]
     full = piece_refs[0].shape[2]
     kv_ref[:, full:] = jnp.zeros((keys, kv_ref.shape[1] - full), jnp.bfloat16)
-    lane = lax.broadcasted_iota(jnp.int32, (rows, keys), 1)
-    key_pos = jnp.zeros((rows, keys), jnp.int32)
-    at = 0
-    for (flip_y, flip_core, flip_head), ref in zip(layout, piece_refs):
-        if flip_y:
-            index, plane = 0, 1 - row
-        else:
-            index = plane = 1 - core if flip_core else 0
-        for step in range(2):
+    firsts = []
+    for step in range(2):
+        for (flip_y, flip_core, flip_head), ref in zip(layout, piece_refs):
+            if flip_y:
+                index, plane = 0, 1 - row
+            else:
+                index = plane = 1 - core if flip_core else 0
+            at = len(firsts) * half_rows
             kv_ref[at : at + half_rows, :full] = ref[index + step]
-            first = half_start(plane + step, flip_y, flip_core, flip_head, rows, half_rows)
-            key_pos = jnp.where(lane >= at, first + lane - at, key_pos)
-            at += half_rows
-    pos = ctx * rows + lax.broadcasted_iota(jnp.int32, (rows, keys), 0)
-    live = (key_pos <= pos) & (key_pos >= begin_of(pos, lengths_ref))
-
+            firsts.append(half_start(plane + step, flip_y, flip_core, flip_head, rows, half_rows))
+    earliest = begin_of(ctx * rows, lengths_ref)
+    older_live = functools.reduce(jnp.maximum, firsts[count:]) + half_rows > earliest
     exponent = scale * math.log2(math.e)
 
     def span(base):
-        return pl.ds(pl.multiple_of(base * rows, rows), SUB * rows)
-
-    def scores(base):
-        return lax.dot_general(
-            q_ref[span(base), :], kv_ref[...], (((1,), (1,)), ((), ())), preferred_element_type=jnp.float32
-        )
-
-    def group(index, carry):
-        subs = SPAN // SUB
-        now = scores(index * SPAN)
-        for sub in range(subs):
-            base = index * SPAN + sub * SUB
-            later = scores(base + SUB) if sub + 1 < subs else None
-            now = jnp.where(live[None], now.reshape(SUB, rows, keys), masked_score)
-            now = now.reshape(SUB * rows, keys)
-            most = jnp.broadcast_to(jnp.max(now, axis=1, keepdims=True), (SUB * rows, 128))
-            if not first_call:
-                before = most_in[span(base), :]
-                most = jnp.maximum(most, before)
-                factor = jnp.exp2((before - most) * exponent)
-            weights = jnp.exp2((now - widen(most, keys // 128)) * exponent)
-            total = jnp.broadcast_to(jnp.sum(weights, axis=1, keepdims=True), (SUB * rows, 128))
-            mixed = jnp.dot(weights.astype(jnp.bfloat16), kv_ref[:, :latent], preferred_element_type=jnp.float32)
+        return slice(base * rows, (base + SUB) * rows)
+
+    def visit(pieces):
+        width = pieces * half_rows
+        lane = lax.broadcasted_iota(jnp.int32, (rows, width), 1)
+        key_pos = lane + firsts[0]
+        for piece in range(1, pieces):
+            at = piece * half_rows
+            key_pos = jnp.where(lane >= at, lane + (firsts[piece] - at), key_pos)
+        pos = ctx * rows + lax.broadcasted_iota(jnp.int32, (rows, width), 0)
+        live = (key_pos <= pos) & (key_pos >= begin_of(pos, lengths_ref))
+
+        def scores(base):
+            return lax.dot_general(
+                q_ref[span(base), :], kv_ref[:width, :], (((1,), (1,)), ((), ())), preferred_element_type=jnp.float32
+            )
+
+        def finish(base, weights, total, most, factor):
+            mixed = jnp.dot(weights, kv_ref[:width, :latent], preferred_element_type=jnp.float32)
             if not first_call:
                 total = total + factor * total_in[span(base), :]
                 mixed = mixed + widen(factor, latent // 128) * sum_in[span(base), :]
@@ -219,12 +214,36 @@
                 sum_out[span(base), :] = mixed
                 most_out[span(base), :] = most
                 total_out[span(base), :] = total
+
+        now = scores(0)
+        waiting = None
+        for base in range(0, heads, SUB):
+            later = scores(base + SUB) if base + SUB < heads else None
+            now = jnp.where(live[None], now.reshape(SUB, rows, width), masked_score).reshape(SUB * rows, width)
+            most = jnp.broadcast_to(jnp.max(now, axis=1, keepdims=True), (SUB * rows, 128))
+            factor = None
+            if not first_call:
+                before = most_in[span(base), :]
+                most = jnp.maximum(most, before)
+                factor = jnp.exp2((before - most) * exponent)
+            weights = jnp.exp2((now - widen(most, width // 128)) * exponent)
+            total = jnp.broadcast_to(jnp.sum(weights, axis=1, keepdims=True), (SUB * rows, 128))
+            if waiting:
+                finish(*waiting)
+            waiting = (base, weights.astype(jnp.bfloat16), total, most, factor)
             now = later
-        return carry
-
-    lax.fori_loop(0, heads // SPAN, group, 0)
+        finish(*waiting)
+
+    @pl.when(older_live)
+    def all_pieces():
+        visit(2 * count)
+
+    @pl.when(jnp.logical_not(older_live))
+    def newer_pieces():
+        visit(count)
+
     if last_call:
-        value_heads(mixed_ref, vu_ref, out_ref)
+        value_heads(mixed_ref, vu_ref, held_ref, out_ref, sems)
 
 
 def params(limit=24):
@@ -301,13 +320,17 @@
         keys = 2 * half_rows * len(pieces)
         scratch = [pltpu.VMEM((keys, wide), jnp.bfloat16)]
         if last:
-            scratch = [pltpu.VMEM((heads * rows, latent), jnp.bfloat16)] + scratch
+            scratch = [
+                pltpu.VMEM((heads * rows, latent), jnp.bfloat16),
+                pltpu.VMEM((rows, heads * value), jnp.bfloat16),
+                pltpu.SemaphoreType.DMA((heads // VALUE_GROUP,)),
+            ] + scratch
         extra = (value_up,) if last else ()
         return pl.pallas_call(
             functools.partial(attend_kernel, layout, scale, not state, last),
             out_shape=jax.ShapeDtypeStruct((rows, heads * value), jnp.bfloat16) if last else state_shape,
             in_specs=[SMEM] + [VMEM] * (1 + len(pieces) + len(state) + len(extra)),
-            out_specs=VMEM if last else [VMEM] * 3,
+            out_specs=HBM if last else [VMEM] * 3,
             scratch_shapes=scratch,
             compiler_params=params(),
             name=next(names),

time: 38.1 us -> 34.9 us (0.916)
  Pallas kernels: 20.5 us -> 14.9 us
  waiting for transfers between devices: 6.67 us -> 8.77 us
    pallas_call x2, Pallas kernels: 16.9 us -> 11.3 us  [attend(): pl.pallas_call(functools.partial(attend_kernel, layout, scale, not state,...]
    ppermute x2, waiting for transfers between devices: 0.01 us -> 2.11 us  [swap_head(): return lax.ppermute(array, 'head', [(0, 1), (1, 0)])]
  transfers between devices with their start and end apart: 9 -> 9, of which waited for: 3 -> 4; matrix products, arithmetic and copies ran while one was open for 0% -> 0% of each run, Pallas kernels for 26% -> 20%
where the time goes in v3:
time: 34.9 us; the launch traced here: 34.6 us
  Pallas kernels  14.9 us (43%)
  starting transfers between devices  10.7 us (31%)
  waiting for transfers between devices  8.77 us (25%)
    pallas_call x2, Pallas kernels, attend(): pl.pallas_call(functools.partial(attend_kernel, layout, scale, not state,...  11.3 us
    ppermute x2, starting transfers between devices, plane_shift(): lax.ppermute(array, 'ctx', [(s, (s + steps) % ctx_size) for s in range(ct...  5.67 us
    ppermute x5, waiting for transfers between devices, swap_ctx(): return lax.ppermute(array, 'ctx', [(s, s ^ bit) for s in range(ctx_size)])  4.35 us
    pallas_call x1, Pallas kernels, shards(): pl.pallas_call(query_kernel, out_shape=(jax.ShapeDtypeStruct((heads * row...  3.27 us
    ppermute x2, starting transfers between devices, swap_head(): return lax.ppermute(array, 'head', [(0, 1), (1, 0)])  2.9 us
    ppermute x2, waiting for transfers between devices, plane_shift(): lax.ppermute(array, 'ctx', [(s, (s + steps) % ctx_size) for s in range(ct...  2.31 us
    ppermute x2, waiting for transfers between devices, swap_head(): return lax.ppermute(array, 'head', [(0, 1), (1, 0)])  2.11 us
    ppermute x5, starting transfers between devices, swap_ctx(): return lax.ppermute(array, 'ctx', [(s, s ^ bit) for s in range(ctx_size)])  2.1 us
  transfers between devices with their start and end apart: 9, of which 4 were waited for; matrix products, arithmetic and copies ran while one was open for 0% of the time, Pallas kernels for 20%

profile of v3, /device:TPU:0, one launch (start us, length us, event | category | flops | bytes accessed | tf_op | source)
XLA Modules:
  0.0 34.6 jit_solution(9412133381715941091)
XLA Ops:
  0.0 0.0 copy-start.1
  0.0 0.0 copy-start.2
  0.0 0.0 copy-start.3
  0.0 3.1 %collective-permute-start = (bf16[64,576]{1,0:T(8,128)(2,1)}, bf16[64,576]{1,0:T(8,128)(2,1)S(1)}, u32[]{:S(2)}, u32[]{:S(2)}) collective-permute-start(bf16[64,576]{1,0:T(8,128)(2,1)} %own_ref.1), channel_id=1, source_target_pairs={{0,8},{2,10},{4,12},{6,14},{8,16},{10,18},{12,20},{14,22},{16,24},... | collective-permute-start | bytes 221192 | tf_op jit(solution)/shard_map/ppermute | solution.py:265
  3.1 2.6 %collective-permute-start.1 = (bf16[64,576]{1,0:T(8,128)(2,1)}, bf16[64,576]{1,0:T(8,128)(2,1)S(1)}, u32[]{:S(2)}, u32[]{:S(2)}) collective-permute-start(bf16[64,576]{1,0:T(8,128)(2,1)} %own_ref.1), channel_id=1, source_target_pairs={{0,16},{2,18},{4,20},{6,22},{8,24},{10,26},{12,28},{14,30},{16,0},... | collective-permute-start | bytes 221192 | tf_op jit(solution)/shard_map/ppermute | solution.py:265
  5.7 3.3 %queries.1 = (bf16[4096,640]{1,0:T(8,128)(2,1)S(1)}, f32[3,64,128]{2,1,0:T(8,128)S(1)}, f32[3,64,128]{2,1,0:T(8,128)S(1)}) custom-call(s32[4]{0:T(128)} %lengths_ref.3, bf16[128,4096]{1,0:T(8,128)(2,1)} %qn_hbm.1, bf16[128,2048]{1,0:T(8,128)(2,1)} %qr_hbm.1, bf16[32,128,512]{2,1,0:T(8,128)(2,1)} %ku_hbm.1), custom_call_target="tpu_custom_call" | custom-call | flops 536870912 | bytes 8388608 | tf_op jit(solution)/shard_map/queries/pallas_call | solution.py:276
  8.9 0.0 copy-start
  9.0 0.0 collective-permute-done.one_ref
  9.0 2.3 %collective-permute-done.1.two_ref = bf16[64,576]{1,0:T(8,128)(2,1)S(1)} collective-permute-done((bf16[64,576]{1,0:T(8,128)(2,1)}, bf16[64,576]{1,0:T(8,128)(2,1)S(1)}, u32[]{:S(2)}, u32[]{:S(2)}) %collective-permute-start.1) | collective-permute-done | bytes 73760 | tf_op jit(solution)/shard_map/ppermute | solution.py:265
  11.3 0.0 copy-done.1
  11.3 0.0 copy-done.3
  11.3 0.4 %rows.1 = (bf16[3,64,576]{2,1,0:T(8,128)(2,1)S(1)}, bf16[2,64,576]{2,1,0:T(8,128)(2,1)S(1)}) custom-call(bf16[64,576]{1,0:T(8,128)(2,1)S(1)} %copy-done.1, bf16[64,576]{1,0:T(8,128)(2,1)S(1)} %collective-permute-done.one_ref, bf16[64,576]{1,0:T(8,128)(2,1)S(1)} %collective-permute-done.1.two_ref, f32[1,512]{1,0:T(1,128)S(1)} %bitcast.1, ...), custom_call_target="tpu_custom_call" | custom-call | tf_op jit(solution)/shard_map/rows/pallas_call | solution.py:296
  11.7 1.6 %collective-permute-start.3 = (bf16[2,64,576]{2,1,0:T(8,128)(2,1)S(1)}, bf16[2,64,576]{2,1,0:T(8,128)(2,1)S(1)}, u32[]{:S(2)}, u32[]{:S(2)}) collective-permute-start(bf16[2,64,576]{2,1,0:T(8,128)(2,1)S(1)} %get-tuple-element.22), channel_id=1, source_target_pairs={{0,4},{2,6},{4,0},{6,2},{8,12},{10,14},{12,8},{14,10},{16,20},{18,... | collective-permute-start | bytes 442376 | tf_op jit(solution)/shard_map/ppermute | solution.py:268
  13.3 0.0 collective-permute-start.5
  13.3 1.5 %collective-permute-start.2 = (bf16[3,64,576]{2,1,0:T(8,128)(2,1)S(1)}, bf16[3,64,576]{2,1,0:T(8,128)(2,1)S(1)}, u32[]{:S(2)}, u32[]{:S(2)}) collective-permute-start(bf16[3,64,576]{2,1,0:T(8,128)(2,1)S(1)} %get-tuple-element.21.refs_0_), channel_id=1, source_target_pairs={{0,1},{1,0},{2,3},{3,2},{4,5},{5,4},{6,7},{7,6},{8,9},{9,8},{10,11... | collective-permute-start | bytes 663560 | tf_op jit(solution)/shard_map/ppermute | solution.py:271
  14.8 3.1 %collective-permute-done.3.refs_2_ = bf16[2,64,576]{2,1,0:T(8,128)(2,1)S(1)} collective-permute-done((bf16[2,64,576]{2,1,0:T(8,128)(2,1)S(1)}, bf16[2,64,576]{2,1,0:T(8,128)(2,1)S(1)}, u32[]{:S(2)}, u32[]{:S(2)}) %collective-permute-start.3) | collective-permute-done | bytes 147488 | tf_op jit(solution)/shard_map/ppermute | solution.py:268
  17.9 0.0 collective-permute-start.6
  17.9 1.4 %collective-permute-start.4 = (bf16[2,64,576]{2,1,0:T(8,128)(2,1)S(1)}, bf16[2,64,576]{2,1,0:T(8,128)(2,1)S(1)}, u32[]{:S(2)}, u32[]{:S(2)}) collective-permute-start(bf16[2,64,576]{2,1,0:T(8,128)(2,1)S(1)} %collective-permute-done.3.refs_2_), channel_id=1, source_target_pairs={{0,1},{1,0},{2,3},{3,2},{4,5},{5,4},{6,7},{7,6},{8,9},{9,8},{10,11... | collective-permute-start | bytes 442376 | tf_op jit(solution)/shard_map/ppermute | solution.py:271
  19.3 0.0 collective-permute-done.5.refs_1_
  19.3 0.0 collective-permute-done.6.refs_3_
  19.3 0.0 copy-done.2
  19.3 3.7 %attend_near.1 = (f32[4096,512]{1,0:T(8,128)S(1)}, f32[4096,128]{1,0:T(8,128)S(1)}, f32[4096,128]{1,0:T(8,128)S(1)}) custom-call(s32[4]{0:T(128)S(1)} %copy-done.2, bf16[4096,640]{1,0:T(8,128)(2,1)S(1)} %get-tuple-element.18.q_ref, bf16[3,64,576]{2,1,0:T(8,128)(2,1)S(1)} %get-tuple-element.21.refs_0_, ...), custom_call_target="tpu_custom_call" | custom-call | tf_op jit(solution)/shard_map/attend_near/pallas_call | solution.py:329
  23.0 0.0 collective-permute-done.2.refs_0_
  23.0 2.1 %collective-permute-done.4.refs_2_ = bf16[2,64,576]{2,1,0:T(8,128)(2,1)S(1)} collective-permute-done((bf16[2,64,576]{2,1,0:T(8,128)(2,1)S(1)}, bf16[2,64,576]{2,1,0:T(8,128)(2,1)S(1)}, u32[]{:S(2)}, u32[]{:S(2)}) %collective-permute-start.4) | collective-permute-done | bytes 147488 | tf_op jit(solution)/shard_map/ppermute | solution.py:271
  25.1 0.0 collective-permute-start.7
  25.1 0.5 %collective-permute-start.8 = (bf16[2,64,576]{2,1,0:T(8,128)(2,1)S(1)}, bf16[2,64,576]{2,1,0:T(8,128)(2,1)S(1)}, u32[]{:S(2)}, u32[]{:S(2)}) collective-permute-start(bf16[2,64,576]{2,1,0:T(8,128)(2,1)S(1)} %collective-permute-done.4.refs_2_), channel_id=1, source_target_pairs={{0,2},{2,0},{4,6},{6,4},{8,10},{10,8},{12,14},{14,12},{16,18},{18,... | collective-permute-start | bytes 442376 | tf_op jit(solution)/shard_map/ppermute | solution.py:268
  25.7 1.2 %collective-permute-done.8.refs_3_ = bf16[2,64,576]{2,1,0:T(8,128)(2,1)S(1)} collective-permute-done((bf16[2,64,576]{2,1,0:T(8,128)(2,1)S(1)}, bf16[2,64,576]{2,1,0:T(8,128)(2,1)S(1)}, u32[]{:S(2)}, u32[]{:S(2)}) %collective-permute-start.8) | collective-permute-done | bytes 147488 | tf_op jit(solution)/shard_map/ppermute | solution.py:268
  26.9 0.0 collective-permute-done.7.refs_1_
  26.9 0.0 copy-done
  26.9 7.5 %attend_far.1 = bf16[128,4096]{1,0:T(8,128)(2,1)} custom-call(s32[4]{0:T(128)S(1)} %copy-done.2, bf16[4096,640]{1,0:T(8,128)(2,1)S(1)} %get-tuple-element.18.q_ref, bf16[3,64,576]{2,1,0:T(8,128)(2,1)S(1)} %collective-permute-done.2.refs_0_, bf16[3,64,576]{2,1,0:T(8,128)(2,1)S(1)} %collective-permute-done.7.refs_1_, ...), custom_call_target="tpu_custom_call" | custom-call | tf_op jit(solution)/shard_map/attend_far/pallas_call | solution.py:329
Async XLA Ops:
  0.0 11.3 %copy-start.1 = (bf16[64,576]{1,0:T(8,128)(2,1)S(1)}, bf16[64,576]{1,0:T(8,128)(2,1)}, u32[]{:S(2)}) copy-start(bf16[64,576]{1,0:T(8,128)(2,1)} %own_ref.1) | copy-start | bytes 221188
  0.0 19.3 %copy-start.2 = (s32[4]{0:T(128)S(1)}, s32[4]{0:T(128)}, u32[]{:S(2)}) copy-start(s32[4]{0:T(128)} %lengths_ref.3) | copy-start | bytes 52
  0.0 11.3 %copy-start.3 = (f32[512]{0:T(512)S(1)}, f32[512]{0:T(512)}, u32[]{:S(2)}) copy-start(f32[512]{0:T(512)} %param.8) | copy-start | bytes 6148
  0.0 9.0 %collective-permute-start = (bf16[64,576]{1,0:T(8,128)(2,1)}, bf16[64,576]{1,0:T(8,128)(2,1)S(1)}, u32[]{:S(2)}, u32[]{:S(2)}) collective-permute-start(bf16[64,576]{1,0:T(8,128)(2,1)} %own_ref.1), channel_id=1, source_target_pairs={{0,8},{2,10},{4,12},{6,14},{8,16},{10,18},{12,20},{14,22},{16,24},... | collective-permute-start | bytes 221192 | tf_op jit(solution)/shard_map/ppermute | solution.py:265
  3.1 8.2 %collective-permute-start.1 = (bf16[64,576]{1,0:T(8,128)(2,1)}, bf16[64,576]{1,0:T(8,128)(2,1)S(1)}, u32[]{:S(2)}, u32[]{:S(2)}) collective-permute-start(bf16[64,576]{1,0:T(8,128)(2,1)} %own_ref.1), channel_id=1, source_target_pairs={{0,16},{2,18},{4,20},{6,22},{8,24},{10,26},{12,28},{14,30},{16,0},... | collective-permute-start | bytes 221192 | tf_op jit(solution)/shard_map/ppermute | solution.py:265
  8.9 17.9 %copy-start = (bf16[32,512,128]{2,1,0:T(8,128)(2,1)S(1)}, bf16[32,512,128]{2,1,0:T(8,128)(2,1)}, u32[]{:S(2)}) copy-start(bf16[32,512,128]{2,1,0:T(8,128)(2,1)} %refs_7_.1) | copy-start | bytes 12582916
  11.7 6.2 %collective-permute-start.3 = (bf16[2,64,576]{2,1,0:T(8,128)(2,1)S(1)}, bf16[2,64,576]{2,1,0:T(8,128)(2,1)S(1)}, u32[]{:S(2)}, u32[]{:S(2)}) collective-permute-start(bf16[2,64,576]{2,1,0:T(8,128)(2,1)S(1)} %get-tuple-element.22), channel_id=1, source_target_pairs={{0,4},{2,6},{4,0},{6,2},{8,12},{10,14},{12,8},{14,10},{16,20},{18,... | collective-permute-start | bytes 442376 | tf_op jit(solution)/shard_map/ppermute | solution.py:268
  13.3 6.0 %collective-permute-start.5 = (bf16[3,64,576]{2,1,0:T(8,128)(2,1)S(1)}, bf16[3,64,576]{2,1,0:T(8,128)(2,1)S(1)}, u32[]{:S(2)}, u32[]{:S(2)}) collective-permute-start(bf16[3,64,576]{2,1,0:T(8,128)(2,1)S(1)} %get-tuple-element.21.refs_0_), channel_id=1, source_target_pairs={{0,2},{2,0},{4,6},{6,4},{8,10},{10,8},{12,14},{14,12},{16,18},{18,... | collective-permute-start | bytes 663560 | tf_op jit(solution)/shard_map/ppermute | solution.py:268
  13.3 9.8 %collective-permute-start.2 = (bf16[3,64,576]{2,1,0:T(8,128)(2,1)S(1)}, bf16[3,64,576]{2,1,0:T(8,128)(2,1)S(1)}, u32[]{:S(2)}, u32[]{:S(2)}) collective-permute-start(bf16[3,64,576]{2,1,0:T(8,128)(2,1)S(1)} %get-tuple-element.21.refs_0_), channel_id=1, source_target_pairs={{0,1},{1,0},{2,3},{3,2},{4,5},{5,4},{6,7},{7,6},{8,9},{9,8},{10,11... | collective-permute-start | bytes 663560 | tf_op jit(solution)/shard_map/ppermute | solution.py:271
  17.9 1.4 %collective-permute-start.6 = (bf16[2,64,576]{2,1,0:T(8,128)(2,1)S(1)}, bf16[2,64,576]{2,1,0:T(8,128)(2,1)S(1)}, u32[]{:S(2)}, u32[]{:S(2)}) collective-permute-start(bf16[2,64,576]{2,1,0:T(8,128)(2,1)S(1)} %collective-permute-done.3.refs_2_), channel_id=1, source_target_pairs={{0,2},{2,0},{4,6},{6,4},{8,10},{10,8},{12,14},{14,12},{16,18},{18,... | collective-permute-start | bytes 442376 | tf_op jit(solution)/shard_map/ppermute | solution.py:268
  17.9 7.3 %collective-permute-start.4 = (bf16[2,64,576]{2,1,0:T(8,128)(2,1)S(1)}, bf16[2,64,576]{2,1,0:T(8,128)(2,1)S(1)}, u32[]{:S(2)}, u32[]{:S(2)}) collective-permute-start(bf16[2,64,576]{2,1,0:T(8,128)(2,1)S(1)} %collective-permute-done.3.refs_2_), channel_id=1, source_target_pairs={{0,1},{1,0},{2,3},{3,2},{4,5},{5,4},{6,7},{7,6},{8,9},{9,8},{10,11... | collective-permute-start | bytes 442376 | tf_op jit(solution)/shard_map/ppermute | solution.py:271
  25.1 1.8 %collective-permute-start.7 = (bf16[3,64,576]{2,1,0:T(8,128)(2,1)S(1)}, bf16[3,64,576]{2,1,0:T(8,128)(2,1)S(1)}, u32[]{:S(2)}, u32[]{:S(2)}) collective-permute-start(bf16[3,64,576]{2,1,0:T(8,128)(2,1)S(1)} %collective-permute-done.2.refs_0_), channel_id=1, source_target_pairs={{0,2},{2,0},{4,6},{6,4},{8,10},{10,8},{12,14},{14,12},{16,18},{18,... | collective-permute-start | bytes 663560 | tf_op jit(solution)/shard_map/ppermute | solution.py:268
  25.1 1.7 %collective-permute-start.8 = (bf16[2,64,576]{2,1,0:T(8,128)(2,1)S(1)}, bf16[2,64,576]{2,1,0:T(8,128)(2,1)S(1)}, u32[]{:S(2)}, u32[]{:S(2)}) collective-permute-start(bf16[2,64,576]{2,1,0:T(8,128)(2,1)S(1)} %collective-permute-done.4.refs_2_), channel_id=1, source_target_pairs={{0,2},{2,0},{4,6},{6,4},{8,10},{10,8},{12,14},{14,12},{16,18},{18,... | collective-permute-start | bytes 442376 | tf_op jit(solution)/shard_map/ppermute | solution.py:268

commit v4 on v3

--- a/solution.py
+++ b/solution.py
@@ -313,7 +313,7 @@
         jax.ShapeDtypeStruct((heads * rows, 128), jnp.float32),
         jax.ShapeDtypeStruct((heads * rows, 128), jnp.float32),
     )
-    names = iter(("attend_near", "attend_far"))
+    names = iter(("attend_near", "attend_across", "attend_far"))
 
     def attend(part, state, last=False):
         pieces, layout = zip(*part)
@@ -332,13 +332,15 @@
             in_specs=[SMEM] + [VMEM] * (1 + len(pieces) + len(state) + len(extra)),
             out_specs=HBM if last else [VMEM] * 3,
             scratch_shapes=scratch,
-            compiler_params=params(),
+            compiler_params=params(18 if last else 8),
             name=next(names),
         )(doc_lengths, queries, *pieces, *state, *extra)
 
+    state = attend(near_pieces, ())
+    across, *state = lax.optimization_barrier((across, *state))
     corner = swap_head(across)
     across_pieces = [(across, (True, False, False)), (swap_ctx(across, 1), (True, True, False))]
-    state = attend(near_pieces + across_pieces, ())
+    state = attend(across_pieces, state)
     side, corner, *state = lax.optimization_barrier((side, corner, *state))
     side_pieces = [(side, (False, False, True)), (swap_ctx(side, 1), (False, True, True))]
     corner_pieces = [(corner, (True, False, True)), (swap_ctx(corner, 1), (True, True, True))]

time: 34.9 us -> 34.7 us (level)
  waiting for transfers between devices: 8.77 us -> 4.7 us
  Pallas kernels: 14.9 us -> 18.7 us
    pallas_call x2 -> x3, Pallas kernels: 11.3 us -> 15.1 us  [attend(): pl.pallas_call(functools.partial(attend_kernel, layout, scale, not state,...]
    ppermute x5, waiting for transfers between devices: 4.35 us -> 1.49 us  [swap_ctx(): return lax.ppermute(array, 'ctx', [(s, s ^ bit) for s in range(ctx_size)])]
    ppermute x2, waiting for transfers between devices: 2.11 us -> 0.88 us  [swap_head(): return lax.ppermute(array, 'head', [(0, 1), (1, 0)])]
  transfers between devices with their start and end apart: 9 -> 9, of which waited for: 4 -> 4; matrix products, arithmetic and copies ran while one was open for 0% -> 0% of each run, Pallas kernels for 20% -> 31%
where the time goes in v4:
time: 34.7 us; the launch traced here: 34.5 us
  Pallas kernels  18.7 us (54%)
  starting transfers between devices  10.8 us (31%)
  waiting for transfers between devices  4.7 us (14%)
    pallas_call x3, Pallas kernels, attend(): pl.pallas_call(functools.partial(attend_kernel, layout, scale, not state,...  15.1 us
    ppermute x2, starting transfers between devices, plane_shift(): lax.ppermute(array, 'ctx', [(s, (s + steps) % ctx_size) for s in range(ct...  5.67 us
    pallas_call x1, Pallas kernels, shards(): pl.pallas_call(query_kernel, out_shape=(jax.ShapeDtypeStruct((heads * row...  3.27 us
    ppermute x2, starting transfers between devices, swap_head(): return lax.ppermute(array, 'head', [(0, 1), (1, 0)])  2.98 us
    ppermute x2, waiting for transfers between devices, plane_shift(): lax.ppermute(array, 'ctx', [(s, (s + steps) % ctx_size) for s in range(ct...  2.33 us
    ppermute x5, starting transfers between devices, swap_ctx(): return lax.ppermute(array, 'ctx', [(s, s ^ bit) for s in range(ctx_size)])  2.18 us
    ppermute x5, waiting for transfers between devices, swap_ctx(): return lax.ppermute(array, 'ctx', [(s, s ^ bit) for s in range(ctx_size)])  1.49 us
    ppermute x2, waiting for transfers between devices, swap_head(): return lax.ppermute(array, 'head', [(0, 1), (1, 0)])  0.88 us
  transfers between devices with their start and end apart: 9, of which 4 were waited for; matrix products, arithmetic and copies ran while one was open for 0% of the time, Pallas kernels for 31%

profile of v4, /device:TPU:0, one launch (start us, length us, event | category | flops | bytes accessed | tf_op | source)
XLA Modules:
  0.0 34.5 jit_solution(6924117318203676087)
XLA Ops:
  0.0 0.0 copy-start.1
  0.0 0.0 copy-start.2
  0.0 0.0 copy-start.3
  0.0 3.1 %collective-permute-start = (bf16[64,576]{1,0:T(8,128)(2,1)}, bf16[64,576]{1,0:T(8,128)(2,1)S(1)}, u32[]{:S(2)}, u32[]{:S(2)}) collective-permute-start(bf16[64,576]{1,0:T(8,128)(2,1)} %own_ref.1), channel_id=1, source_target_pairs={{0,8},{2,10},{4,12},{6,14},{8,16},{10,18},{12,20},{14,22},{16,24},... | collective-permute-start | bytes 221192 | tf_op jit(solution)/shard_map/ppermute | solution.py:265
  3.1 2.6 %collective-permute-start.1 = (bf16[64,576]{1,0:T(8,128)(2,1)}, bf16[64,576]{1,0:T(8,128)(2,1)S(1)}, u32[]{:S(2)}, u32[]{:S(2)}) collective-permute-start(bf16[64,576]{1,0:T(8,128)(2,1)} %own_ref.1), channel_id=1, source_target_pairs={{0,16},{2,18},{4,20},{6,22},{8,24},{10,26},{12,28},{14,30},{16,0},... | collective-permute-start | bytes 221192 | tf_op jit(solution)/shard_map/ppermute | solution.py:265
  5.7 3.3 %queries.1 = (bf16[4096,640]{1,0:T(8,128)(2,1)S(1)}, f32[3,64,128]{2,1,0:T(8,128)S(1)}, f32[3,64,128]{2,1,0:T(8,128)S(1)}) custom-call(s32[4]{0:T(128)} %lengths_ref.5, bf16[128,4096]{1,0:T(8,128)(2,1)} %qn_hbm.1, bf16[128,2048]{1,0:T(8,128)(2,1)} %qr_hbm.1, bf16[32,128,512]{2,1,0:T(8,128)(2,1)} %ku_hbm.1), custom_call_target="tpu_custom_call" | custom-call | flops 536870912 | bytes 8388608 | tf_op jit(solution)/shard_map/queries/pallas_call | solution.py:276
  8.9 0.0 collective-permute-done.one_ref
  9.0 2.3 %collective-permute-done.1.two_ref = bf16[64,576]{1,0:T(8,128)(2,1)S(1)} collective-permute-done((bf16[64,576]{1,0:T(8,128)(2,1)}, bf16[64,576]{1,0:T(8,128)(2,1)S(1)}, u32[]{:S(2)}, u32[]{:S(2)}) %collective-permute-start.1) | collective-permute-done | bytes 73760 | tf_op jit(solution)/shard_map/ppermute | solution.py:265
  11.3 0.0 copy-done.1
  11.3 0.0 copy-done.3
  11.3 0.4 %rows.1 = (bf16[3,64,576]{2,1,0:T(8,128)(2,1)S(1)}, bf16[2,64,576]{2,1,0:T(8,128)(2,1)S(1)}) custom-call(bf16[64,576]{1,0:T(8,128)(2,1)S(1)} %copy-done.1, bf16[64,576]{1,0:T(8,128)(2,1)S(1)} %collective-permute-done.one_ref, bf16[64,576]{1,0:T(8,128)(2,1)S(1)} %collective-permute-done.1.two_ref, f32[1,512]{1,0:T(1,128)S(1)} %bitcast.1, ...), custom_call_target="tpu_custom_call" | custom-call | tf_op jit(solution)/shard_map/rows/pallas_call | solution.py:296
  11.7 0.1 collective-permute-start.4
  11.8 1.6 %collective-permute-start.3 = (bf16[2,64,576]{2,1,0:T(8,128)(2,1)S(1)}, bf16[2,64,576]{2,1,0:T(8,128)(2,1)S(1)}, u32[]{:S(2)}, u32[]{:S(2)}) collective-permute-start(bf16[2,64,576]{2,1,0:T(8,128)(2,1)S(1)} %get-tuple-element.29), channel_id=1, source_target_pairs={{0,4},{2,6},{4,0},{6,2},{8,12},{10,14},{12,8},{14,10},{16,20},{18,... | collective-permute-start | bytes 442376 | tf_op jit(solution)/shard_map/ppermute | solution.py:268
  13.3 1.5 %collective-permute-start.2 = (bf16[3,64,576]{2,1,0:T(8,128)(2,1)S(1)}, bf16[3,64,576]{2,1,0:T(8,128)(2,1)S(1)}, u32[]{:S(2)}, u32[]{:S(2)}) collective-permute-start(bf16[3,64,576]{2,1,0:T(8,128)(2,1)S(1)} %get-tuple-element.28.refs_0_), channel_id=1, source_target_pairs={{0,1},{1,0},{2,3},{3,2},{4,5},{5,4},{6,7},{7,6},{8,9},{9,8},{10,11... | collective-permute-start | bytes 663560 | tf_op jit(solution)/shard_map/ppermute | solution.py:271
  14.8 0.0 collective-permute-done.4.refs_1_
  14.8 0.0 copy-done.2
  14.8 3.3 %attend_near.1 = (f32[4096,512]{1,0:T(8,128)S(1)}, f32[4096,128]{1,0:T(8,128)S(1)}, f32[4096,128]{1,0:T(8,128)S(1)}) custom-call(s32[4]{0:T(128)S(1)} %copy-done.2, bf16[4096,640]{1,0:T(8,128)(2,1)S(1)} %get-tuple-element.25.q_ref, bf16[3,64,576]{2,1,0:T(8,128)(2,1)S(1)} %get-tuple-element.28.refs_0_, bf16[3,64,576]{2,1,0:T(8,128)(2,1)S(1)} %collective-permute-done.4.refs_1_), custom_call_target="tpu_custom_call" | custom-call | tf_op jit(solution)/shard_map/attend_near/pallas_call | solution.py:329
  18.1 0.2 collective-permute-done.3.refs_0_
  18.4 0.0 copy-start
  18.4 0.0 collective-permute-start.6
  18.4 1.5 %collective-permute-start.5 = (bf16[2,64,576]{2,1,0:T(8,128)(2,1)S(1)}, bf16[2,64,576]{2,1,0:T(8,128)(2,1)S(1)}, u32[]{:S(2)}, u32[]{:S(2)}) collective-permute-start(bf16[2,64,576]{2,1,0:T(8,128)(2,1)S(1)} %collective-permute-done.3.refs_0_), channel_id=1, source_target_pairs={{0,1},{1,0},{2,3},{3,2},{4,5},{5,4},{6,7},{7,6},{8,9},{9,8},{10,11... | collective-permute-start | bytes 442376 | tf_op jit(solution)/shard_map/ppermute | solution.py:271
  19.9 0.0 collective-permute-done.6.refs_1_
  19.9 4.2 %attend_across.1 = (f32[4096,512]{1,0:T(8,128)S(1)}, f32[4096,128]{1,0:T(8,128)S(1)}, f32[4096,128]{1,0:T(8,128)S(1)}) custom-call(s32[4]{0:T(128)S(1)} %copy-done.2, bf16[4096,640]{1,0:T(8,128)(2,1)S(1)} %get-tuple-element.25.q_ref, bf16[2,64,576]{2,1,0:T(8,128)(2,1)S(1)} %collective-permute-done.3.refs_0_, ...), custom_call_target="tpu_custom_call" | custom-call | tf_op jit(solution)/shard_map/attend_across/pallas_call | solution.py:329
  24.1 0.0 collective-permute-done.2.refs_0_
  24.1 0.9 %collective-permute-done.5.refs_2_ = bf16[2,64,576]{2,1,0:T(8,128)(2,1)S(1)} collective-permute-done((bf16[2,64,576]{2,1,0:T(8,128)(2,1)S(1)}, bf16[2,64,576]{2,1,0:T(8,128)(2,1)S(1)}, u32[]{:S(2)}, u32[]{:S(2)}) %collective-permute-start.5) | collective-permute-done | bytes 147488 | tf_op jit(solution)/shard_map/ppermute | solution.py:271
  25.0 0.0 collective-permute-start.7
  25.0 0.5 %collective-permute-start.8 = (bf16[2,64,576]{2,1,0:T(8,128)(2,1)S(1)}, bf16[2,64,576]{2,1,0:T(8,128)(2,1)S(1)}, u32[]{:S(2)}, u32[]{:S(2)}) collective-permute-start(bf16[2,64,576]{2,1,0:T(8,128)(2,1)S(1)} %collective-permute-done.5.refs_2_), channel_id=1, source_target_pairs={{0,2},{2,0},{4,6},{6,4},{8,10},{10,8},{12,14},{14,12},{16,18},{18,... | collective-permute-start | bytes 442376 | tf_op jit(solution)/shard_map/ppermute | solution.py:268
  25.5 1.2 %collective-permute-done.8.refs_3_ = bf16[2,64,576]{2,1,0:T(8,128)(2,1)S(1)} collective-permute-done((bf16[2,64,576]{2,1,0:T(8,128)(2,1)S(1)}, bf16[2,64,576]{2,1,0:T(8,128)(2,1)S(1)}, u32[]{:S(2)}, u32[]{:S(2)}) %collective-permute-start.8) | collective-permute-done | bytes 147488 | tf_op jit(solution)/shard_map/ppermute | solution.py:268
  26.7 0.0 collective-permute-done.7.refs_1_
  26.7 0.0 copy-done
  26.7 7.6 %attend_far.1 = bf16[128,4096]{1,0:T(8,128)(2,1)} custom-call(s32[4]{0:T(128)S(1)} %copy-done.2, bf16[4096,640]{1,0:T(8,128)(2,1)S(1)} %get-tuple-element.25.q_ref, bf16[3,64,576]{2,1,0:T(8,128)(2,1)S(1)} %collective-permute-done.2.refs_0_, bf16[3,64,576]{2,1,0:T(8,128)(2,1)S(1)} %collective-permute-done.7.refs_1_, ...), custom_call_target="tpu_custom_call" | custom-call | tf_op jit(solution)/shard_map/attend_far/pallas_call | solution.py:329
Async XLA Ops:
  0.0 11.3 %copy-start.1 = (bf16[64,576]{1,0:T(8,128)(2,1)S(1)}, bf16[64,576]{1,0:T(8,128)(2,1)}, u32[]{:S(2)}) copy-start(bf16[64,576]{1,0:T(8,128)(2,1)} %own_ref.1) | copy-start | bytes 221188
  0.0 14.8 %copy-start.2 = (s32[4]{0:T(128)S(1)}, s32[4]{0:T(128)}, u32[]{:S(2)}) copy-start(s32[4]{0:T(128)} %lengths_ref.5) | copy-start | bytes 52
  0.0 11.3 %copy-start.3 = (f32[512]{0:T(512)S(1)}, f32[512]{0:T(512)}, u32[]{:S(2)}) copy-start(f32[512]{0:T(512)} %param.8) | copy-start | bytes 6148
  0.0 8.9 %collective-permute-start = (bf16[64,576]{1,0:T(8,128)(2,1)}, bf16[64,576]{1,0:T(8,128)(2,1)S(1)}, u32[]{:S(2)}, u32[]{:S(2)}) collective-permute-start(bf16[64,576]{1,0:T(8,128)(2,1)} %own_ref.1), channel_id=1, source_target_pairs={{0,8},{2,10},{4,12},{6,14},{8,16},{10,18},{12,20},{14,22},{16,24},... | collective-permute-start | bytes 221192 | tf_op jit(solution)/shard_map/ppermute | solution.py:265
  3.1 8.2 %collective-permute-start.1 = (bf16[64,576]{1,0:T(8,128)(2,1)}, bf16[64,576]{1,0:T(8,128)(2,1)S(1)}, u32[]{:S(2)}, u32[]{:S(2)}) collective-permute-start(bf16[64,576]{1,0:T(8,128)(2,1)} %own_ref.1), channel_id=1, source_target_pairs={{0,16},{2,18},{4,20},{6,22},{8,24},{10,26},{12,28},{14,30},{16,0},... | collective-permute-start | bytes 221192 | tf_op jit(solution)/shard_map/ppermute | solution.py:265
  11.7 3.2 %collective-permute-start.4 = (bf16[3,64,576]{2,1,0:T(8,128)(2,1)S(1)}, bf16[3,64,576]{2,1,0:T(8,128)(2,1)S(1)}, u32[]{:S(2)}, u32[]{:S(2)}) collective-permute-start(bf16[3,64,576]{2,1,0:T(8,128)(2,1)S(1)} %get-tuple-element.28.refs_0_), channel_id=1, source_target_pairs={{0,2},{2,0},{4,6},{6,4},{8,10},{10,8},{12,14},{14,12},{16,18},{18,... | collective-permute-start | bytes 663560 | tf_op jit(solution)/shard_map/ppermute | solution.py:268
  11.8 6.6 %collective-permute-start.3 = (bf16[2,64,576]{2,1,0:T(8,128)(2,1)S(1)}, bf16[2,64,576]{2,1,0:T(8,128)(2,1)S(1)}, u32[]{:S(2)}, u32[]{:S(2)}) collective-permute-start(bf16[2,64,576]{2,1,0:T(8,128)(2,1)S(1)} %get-tuple-element.29), channel_id=1, source_target_pairs={{0,4},{2,6},{4,0},{6,2},{8,12},{10,14},{12,8},{14,10},{16,20},{18,... | collective-permute-start | bytes 442376 | tf_op jit(solution)/shard_map/ppermute | solution.py:268
  13.3 10.8 %collective-permute-start.2 = (bf16[3,64,576]{2,1,0:T(8,128)(2,1)S(1)}, bf16[3,64,576]{2,1,0:T(8,128)(2,1)S(1)}, u32[]{:S(2)}, u32[]{:S(2)}) collective-permute-start(bf16[3,64,576]{2,1,0:T(8,128)(2,1)S(1)} %get-tuple-element.28.refs_0_), channel_id=1, source_target_pairs={{0,1},{1,0},{2,3},{3,2},{4,5},{5,4},{6,7},{7,6},{8,9},{9,8},{10,11... | collective-permute-start | bytes 663560 | tf_op jit(solution)/shard_map/ppermute | solution.py:271
  18.4 8.4 %copy-start = (bf16[32,512,128]{2,1,0:T(8,128)(2,1)S(1)}, bf16[32,512,128]{2,1,0:T(8,128)(2,1)}, u32[]{:S(2)}) copy-start(bf16[32,512,128]{2,1,0:T(8,128)(2,1)} %refs_7_.1) | copy-start | bytes 12582916
  18.4 1.5 %collective-permute-start.6 = (bf16[2,64,576]{2,1,0:T(8,128)(2,1)S(1)}, bf16[2,64,576]{2,1,0:T(8,128)(2,1)S(1)}, u32[]{:S(2)}, u32[]{:S(2)}) collective-permute-start(bf16[2,64,576]{2,1,0:T(8,128)(2,1)S(1)} %collective-permute-done.3.refs_0_), channel_id=1, source_target_pairs={{0,2},{2,0},{4,6},{6,4},{8,10},{10,8},{12,14},{14,12},{16,18},{18,... | collective-permute-start | bytes 442376 | tf_op jit(solution)/shard_map/ppermute | solution.py:268
  18.4 6.6 %collective-permute-start.5 = (bf16[2,64,576]{2,1,0:T(8,128)(2,1)S(1)}, bf16[2,64,576]{2,1,0:T(8,128)(2,1)S(1)}, u32[]{:S(2)}, u32[]{:S(2)}) collective-permute-start(bf16[2,64,576]{2,1,0:T(8,128)(2,1)S(1)} %collective-permute-done.3.refs_0_), channel_id=1, source_target_pairs={{0,1},{1,0},{2,3},{3,2},{4,5},{5,4},{6,7},{7,6},{8,9},{9,8},{10,11... | collective-permute-start | bytes 442376 | tf_op jit(solution)/shard_map/ppermute | solution.py:271
  25.0 1.8 %collective-permute-start.7 = (bf16[3,64,576]{2,1,0:T(8,128)(2,1)S(1)}, bf16[3,64,576]{2,1,0:T(8,128)(2,1)S(1)}, u32[]{:S(2)}, u32[]{:S(2)}) collective-permute-start(bf16[3,64,576]{2,1,0:T(8,128)(2,1)S(1)} %collective-permute-done.2.refs_0_), channel_id=1, source_target_pairs={{0,2},{2,0},{4,6},{6,4},{8,10},{10,8},{12,14},{14,12},{16,18},{18,... | collective-permute-start | bytes 663560 | tf_op jit(solution)/shard_map/ppermute | solution.py:268
  25.0 1.7 %collective-permute-start.8 = (bf16[2,64,576]{2,1,0:T(8,128)(2,1)S(1)}, bf16[2,64,576]{2,1,0:T(8,128)(2,1)S(1)}, u32[]{:S(2)}, u32[]{:S(2)}) collective-permute-start(bf16[2,64,576]{2,1,0:T(8,128)(2,1)S(1)} %collective-permute-done.5.refs_2_), channel_id=1, source_target_pairs={{0,2},{2,0},{4,6},{6,4},{8,10},{10,8},{12,14},{14,12},{16,18},{18,... | collective-permute-start | bytes 442376 | tf_op jit(solution)/shard_map/ppermute | solution.py:268

commit v5 on v4

--- a/solution.py
+++ b/solution.py
@@ -130,23 +130,20 @@
     return jnp.concatenate([column] * count, axis=1)
 
 
-def value_heads(mixed_ref, vu_ref, held_ref, out_ref, sems):
-    heads, latent, value = vu_ref.shape
+def value_heads(base, mixed, vu_ref, held_ref, out_ref, sems):
+    value = vu_ref.shape[2]
     rows = held_ref.shape[0]
-    copies = []
-    for head in range(heads):
-        cols = slice(head * value, (head + 1) * value)
-        result = jnp.dot(
-            mixed_ref[head * rows : (head + 1) * rows, :], vu_ref[head], preferred_element_type=jnp.float32
-        )
+    for j in range(SUB):
+        cols = slice((base + j) * value, (base + j + 1) * value)
+        result = jnp.dot(mixed[j * rows : (j + 1) * rows], vu_ref[base + j], preferred_element_type=jnp.float32)
         held_ref[:, cols] = result.astype(jnp.bfloat16)
-        if (head + 1) % VALUE_GROUP == 0:
-            group = head // VALUE_GROUP
-            cols = slice(group * VALUE_GROUP * value, (head + 1) * value)
-            copies.append(pltpu.make_async_copy(held_ref.at[:, cols], out_ref.at[:, cols], sems.at[group]))
-            copies[-1].start()
-    for copy in copies:
-        copy.wait()
+    if (base + SUB) % VALUE_GROUP:
+        return []
+    group = base // VALUE_GROUP
+    cols = slice(group * VALUE_GROUP * value, (base + SUB) * value)
+    copy = pltpu.make_async_copy(held_ref.at[:, cols], out_ref.at[:, cols], sems.at[group])
+    copy.start()
+    return [copy]
 
 
 def attend_kernel(layout, scale, first_call, last_call, lengths_ref, q_ref, *refs):
@@ -156,8 +153,8 @@
         sum_in, most_in, total_in = refs[:3]
         refs = refs[3:]
     if last_call:
-        vu_ref, out_ref, mixed_ref, held_ref, sems, kv_ref = refs
-        latent = mixed_ref.shape[1]
+        vu_ref, out_ref, held_ref, sems, kv_ref = refs
+        latent = vu_ref.shape[1]
     else:
         sum_out, most_out, total_out, kv_ref = refs
         latent = sum_out.shape[1]
@@ -209,12 +206,13 @@
                 mixed = mixed + widen(factor, latent // 128) * sum_in[span(base), :]
             if last_call:
                 mixed = mixed * widen(1.0 / total, latent // 128)
-                mixed_ref[span(base), :] = mixed.astype(jnp.bfloat16)
+                copies.extend(value_heads(base, mixed.astype(jnp.bfloat16), vu_ref, held_ref, out_ref, sems))
             else:
                 sum_out[span(base), :] = mixed
                 most_out[span(base), :] = most
                 total_out[span(base), :] = total
 
+        copies = []
         now = scores(0)
         waiting = None
         for base in range(0, heads, SUB):
@@ -233,6 +231,8 @@
             waiting = (base, weights.astype(jnp.bfloat16), total, most, factor)
             now = later
         finish(*waiting)
+        for copy in copies:
+            copy.wait()
 
     @pl.when(older_live)
     def all_pieces():
@@ -241,9 +241,6 @@
     @pl.when(jnp.logical_not(older_live))
     def newer_pieces():
         visit(count)
-
-    if last_call:
-        value_heads(mixed_ref, vu_ref, held_ref, out_ref, sems)
 
 
 def params(limit=24):
@@ -321,7 +318,6 @@
         scratch = [pltpu.VMEM((keys, wide), jnp.bfloat16)]
         if last:
             scratch = [
-                pltpu.VMEM((heads * rows, latent), jnp.bfloat16),
                 pltpu.VMEM((rows, heads * value), jnp.bfloat16),
                 pltpu.SemaphoreType.DMA((heads // VALUE_GROUP,)),
             ] + scratch

time: 34.7 us -> 34.2 us (0.986)
  Pallas kernels: 18.7 us -> 18 us
    pallas_call x3, Pallas kernels: 15.1 us -> 14.4 us  [attend(): pl.pallas_call(functools.partial(attend_kernel, layout, scale, not state,...]
  transfers between devices with their start and end apart: 9 -> 9, of which waited for: 4 -> 4; matrix products, arithmetic and copies ran while one was open for 0% -> 0% of each run, Pallas kernels for 31% -> 32%
where the time goes in v5:
time: 34.2 us; the launch traced here: 33.8 us
  Pallas kernels  18 us (53%)
  starting transfers between devices  10.8 us (32%)
  waiting for transfers between devices  4.7 us (14%)
    pallas_call x3, Pallas kernels, attend(): pl.pallas_call(functools.partial(attend_kernel, layout, scale, not state,...  14.4 us
    ppermute x2, starting transfers between devices, plane_shift(): lax.ppermute(array, 'ctx', [(s, (s + steps) % ctx_size) for s in range(ct...  5.67 us
    pallas_call x1, Pallas kernels, shards(): pl.pallas_call(query_kernel, out_shape=(jax.ShapeDtypeStruct((heads * row...  3.27 us
    ppermute x2, starting transfers between devices, swap_head(): return lax.ppermute(array, 'head', [(0, 1), (1, 0)])  2.98 us
    ppermute x2, waiting for transfers between devices, plane_shift(): lax.ppermute(array, 'ctx', [(s, (s + steps) % ctx_size) for s in range(ct...  2.33 us
    ppermute x5, starting transfers between devices, swap_ctx(): return lax.ppermute(array, 'ctx', [(s, s ^ bit) for s in range(ctx_size)])  2.18 us
    ppermute x5, waiting for transfers between devices, swap_ctx(): return lax.ppermute(array, 'ctx', [(s, s ^ bit) for s in range(ctx_size)])  1.49 us
    ppermute x2, waiting for transfers between devices, swap_head(): return lax.ppermute(array, 'head', [(0, 1), (1, 0)])  0.88 us
  transfers between devices with their start and end apart: 9, of which 4 were waited for; matrix products, arithmetic and copies ran while one was open for 0% of the time, Pallas kernels for 32%

profile of v5, /device:TPU:0, one launch (start us, length us, event | category | flops | bytes accessed | tf_op | source)
XLA Modules:
  0.0 33.8 jit_solution(2527912802497390688)
XLA Ops:
  0.0 0.0 copy-start.1
  0.0 0.0 copy-start.2
  0.0 0.0 copy-start.3
  0.0 3.1 %collective-permute-start = (bf16[64,576]{1,0:T(8,128)(2,1)}, bf16[64,576]{1,0:T(8,128)(2,1)S(1)}, u32[]{:S(2)}, u32[]{:S(2)}) collective-permute-start(bf16[64,576]{1,0:T(8,128)(2,1)} %own_ref.1), channel_id=1, source_target_pairs={{0,8},{2,10},{4,12},{6,14},{8,16},{10,18},{12,20},{14,22},{16,24},... | collective-permute-start | bytes 221192 | tf_op jit(solution)/shard_map/ppermute | solution.py:262
  3.1 2.6 %collective-permute-start.1 = (bf16[64,576]{1,0:T(8,128)(2,1)}, bf16[64,576]{1,0:T(8,128)(2,1)S(1)}, u32[]{:S(2)}, u32[]{:S(2)}) collective-permute-start(bf16[64,576]{1,0:T(8,128)(2,1)} %own_ref.1), channel_id=1, source_target_pairs={{0,16},{2,18},{4,20},{6,22},{8,24},{10,26},{12,28},{14,30},{16,0},... | collective-permute-start | bytes 221192 | tf_op jit(solution)/shard_map/ppermute | solution.py:262
  5.7 3.3 %queries.1 = (bf16[4096,640]{1,0:T(8,128)(2,1)S(1)}, f32[3,64,128]{2,1,0:T(8,128)S(1)}, f32[3,64,128]{2,1,0:T(8,128)S(1)}) custom-call(s32[4]{0:T(128)} %lengths_ref.5, bf16[128,4096]{1,0:T(8,128)(2,1)} %qn_hbm.1, bf16[128,2048]{1,0:T(8,128)(2,1)} %qr_hbm.1, bf16[32,128,512]{2,1,0:T(8,128)(2,1)} %ku_hbm.1), custom_call_target="tpu_custom_call" | custom-call | flops 536870912 | bytes 8388608 | tf_op jit(solution)/shard_map/queries/pallas_call | solution.py:273
  8.9 0.0 collective-permute-done.one_ref
  9.0 2.3 %collective-permute-done.1.two_ref = bf16[64,576]{1,0:T(8,128)(2,1)S(1)} collective-permute-done((bf16[64,576]{1,0:T(8,128)(2,1)}, bf16[64,576]{1,0:T(8,128)(2,1)S(1)}, u32[]{:S(2)}, u32[]{:S(2)}) %collective-permute-start.1) | collective-permute-done | bytes 73760 | tf_op jit(solution)/shard_map/ppermute | solution.py:262
  11.3 0.0 copy-done.1
  11.3 0.0 copy-done.3
  11.3 0.4 %rows.1 = (bf16[3,64,576]{2,1,0:T(8,128)(2,1)S(1)}, bf16[2,64,576]{2,1,0:T(8,128)(2,1)S(1)}) custom-call(bf16[64,576]{1,0:T(8,128)(2,1)S(1)} %copy-done.1, bf16[64,576]{1,0:T(8,128)(2,1)S(1)} %collective-permute-done.one_ref, bf16[64,576]{1,0:T(8,128)(2,1)S(1)} %collective-permute-done.1.two_ref, f32[1,512]{1,0:T(1,128)S(1)} %bitcast.1, ...), custom_call_target="tpu_custom_call" | custom-call | tf_op jit(solution)/shard_map/rows/pallas_call | solution.py:293
  11.7 0.1 collective-permute-start.4
  11.8 1.6 %collective-permute-start.3 = (bf16[2,64,576]{2,1,0:T(8,128)(2,1)S(1)}, bf16[2,64,576]{2,1,0:T(8,128)(2,1)S(1)}, u32[]{:S(2)}, u32[]{:S(2)}) collective-permute-start(bf16[2,64,576]{2,1,0:T(8,128)(2,1)S(1)} %get-tuple-element.29), channel_id=1, source_target_pairs={{0,4},{2,6},{4,0},{6,2},{8,12},{10,14},{12,8},{14,10},{16,20},{18,... | collective-permute-start | bytes 442376 | tf_op jit(solution)/shard_map/ppermute | solution.py:265
  13.3 1.5 %collective-permute-start.2 = (bf16[3,64,576]{2,1,0:T(8,128)(2,1)S(1)}, bf16[3,64,576]{2,1,0:T(8,128)(2,1)S(1)}, u32[]{:S(2)}, u32[]{:S(2)}) collective-permute-start(bf16[3,64,576]{2,1,0:T(8,128)(2,1)S(1)} %get-tuple-element.28.refs_0_), channel_id=1, source_target_pairs={{0,1},{1,0},{2,3},{3,2},{4,5},{5,4},{6,7},{7,6},{8,9},{9,8},{10,11... | collective-permute-start | bytes 663560 | tf_op jit(solution)/shard_map/ppermute | solution.py:268
  14.8 0.0 collective-permute-done.4.refs_1_
  14.8 0.0 copy-done.2
  14.8 3.3 %attend_near.1 = (f32[4096,512]{1,0:T(8,128)S(1)}, f32[4096,128]{1,0:T(8,128)S(1)}, f32[4096,128]{1,0:T(8,128)S(1)}) custom-call(s32[4]{0:T(128)S(1)} %copy-done.2, bf16[4096,640]{1,0:T(8,128)(2,1)S(1)} %get-tuple-element.25.q_ref, bf16[3,64,576]{2,1,0:T(8,128)(2,1)S(1)} %get-tuple-element.28.refs_0_, bf16[3,64,576]{2,1,0:T(8,128)(2,1)S(1)} %collective-permute-done.4.refs_1_), custom_call_target="tpu_custom_call" | custom-call | tf_op jit(solution)/shard_map/attend_near/pallas_call | solution.py:325
  18.1 0.2 collective-permute-done.3.refs_0_
  18.4 0.0 copy-start
  18.4 0.0 collective-permute-start.6
  18.4 1.5 %collective-permute-start.5 = (bf16[2,64,576]{2,1,0:T(8,128)(2,1)S(1)}, bf16[2,64,576]{2,1,0:T(8,128)(2,1)S(1)}, u32[]{:S(2)}, u32[]{:S(2)}) collective-permute-start(bf16[2,64,576]{2,1,0:T(8,128)(2,1)S(1)} %collective-permute-done.3.refs_0_), channel_id=1, source_target_pairs={{0,1},{1,0},{2,3},{3,2},{4,5},{5,4},{6,7},{7,6},{8,9},{9,8},{10,11... | collective-permute-start | bytes 442376 | tf_op jit(solution)/shard_map/ppermute | solution.py:268
  19.9 0.0 collective-permute-done.6.refs_1_
  19.9 4.2 %attend_across.1 = (f32[4096,512]{1,0:T(8,128)S(1)}, f32[4096,128]{1,0:T(8,128)S(1)}, f32[4096,128]{1,0:T(8,128)S(1)}) custom-call(s32[4]{0:T(128)S(1)} %copy-done.2, bf16[4096,640]{1,0:T(8,128)(2,1)S(1)} %get-tuple-element.25.q_ref, bf16[2,64,576]{2,1,0:T(8,128)(2,1)S(1)} %collective-permute-done.3.refs_0_, ...), custom_call_target="tpu_custom_call" | custom-call | tf_op jit(solution)/shard_map/attend_across/pallas_call | solution.py:325
  24.1 0.0 collective-permute-done.2.refs_0_
  24.1 0.9 %collective-permute-done.5.refs_2_ = bf16[2,64,576]{2,1,0:T(8,128)(2,1)S(1)} collective-permute-done((bf16[2,64,576]{2,1,0:T(8,128)(2,1)S(1)}, bf16[2,64,576]{2,1,0:T(8,128)(2,1)S(1)}, u32[]{:S(2)}, u32[]{:S(2)}) %collective-permute-start.5) | collective-permute-done | bytes 147488 | tf_op jit(solution)/shard_map/ppermute | solution.py:268
  25.0 0.0 collective-permute-start.7
  25.0 0.5 %collective-permute-start.8 = (bf16[2,64,576]{2,1,0:T(8,128)(2,1)S(1)}, bf16[2,64,576]{2,1,0:T(8,128)(2,1)S(1)}, u32[]{:S(2)}, u32[]{:S(2)}) collective-permute-start(bf16[2,64,576]{2,1,0:T(8,128)(2,1)S(1)} %collective-permute-done.5.refs_2_), channel_id=1, source_target_pairs={{0,2},{2,0},{4,6},{6,4},{8,10},{10,8},{12,14},{14,12},{16,18},{18,... | collective-permute-start | bytes 442376 | tf_op jit(solution)/shard_map/ppermute | solution.py:265
  25.5 1.2 %collective-permute-done.8.refs_3_ = bf16[2,64,576]{2,1,0:T(8,128)(2,1)S(1)} collective-permute-done((bf16[2,64,576]{2,1,0:T(8,128)(2,1)S(1)}, bf16[2,64,576]{2,1,0:T(8,128)(2,1)S(1)}, u32[]{:S(2)}, u32[]{:S(2)}) %collective-permute-start.8) | collective-permute-done | bytes 147488 | tf_op jit(solution)/shard_map/ppermute | solution.py:265
  26.7 0.0 collective-permute-done.7.refs_1_
  26.7 0.0 copy-done
  26.7 6.9 %attend_far.1 = bf16[128,4096]{1,0:T(8,128)(2,1)} custom-call(s32[4]{0:T(128)S(1)} %copy-done.2, bf16[4096,640]{1,0:T(8,128)(2,1)S(1)} %get-tuple-element.25.q_ref, bf16[3,64,576]{2,1,0:T(8,128)(2,1)S(1)} %collective-permute-done.2.refs_0_, bf16[3,64,576]{2,1,0:T(8,128)(2,1)S(1)} %collective-permute-done.7.refs_1_, ...), custom_call_target="tpu_custom_call" | custom-call | tf_op jit(solution)/shard_map/attend_far/pallas_call | solution.py:325
Async XLA Ops:
  0.0 11.3 %copy-start.1 = (bf16[64,576]{1,0:T(8,128)(2,1)S(1)}, bf16[64,576]{1,0:T(8,128)(2,1)}, u32[]{:S(2)}) copy-start(bf16[64,576]{1,0:T(8,128)(2,1)} %own_ref.1) | copy-start | bytes 221188
  0.0 14.8 %copy-start.2 = (s32[4]{0:T(128)S(1)}, s32[4]{0:T(128)}, u32[]{:S(2)}) copy-start(s32[4]{0:T(128)} %lengths_ref.5) | copy-start | bytes 52
  0.0 11.3 %copy-start.3 = (f32[512]{0:T(512)S(1)}, f32[512]{0:T(512)}, u32[]{:S(2)}) copy-start(f32[512]{0:T(512)} %param.8) | copy-start | bytes 6148
  0.0 8.9 %collective-permute-start = (bf16[64,576]{1,0:T(8,128)(2,1)}, bf16[64,576]{1,0:T(8,128)(2,1)S(1)}, u32[]{:S(2)}, u32[]{:S(2)}) collective-permute-start(bf16[64,576]{1,0:T(8,128)(2,1)} %own_ref.1), channel_id=1, source_target_pairs={{0,8},{2,10},{4,12},{6,14},{8,16},{10,18},{12,20},{14,22},{16,24},... | collective-permute-start | bytes 221192 | tf_op jit(solution)/shard_map/ppermute | solution.py:262
  3.1 8.2 %collective-permute-start.1 = (bf16[64,576]{1,0:T(8,128)(2,1)}, bf16[64,576]{1,0:T(8,128)(2,1)S(1)}, u32[]{:S(2)}, u32[]{:S(2)}) collective-permute-start(bf16[64,576]{1,0:T(8,128)(2,1)} %own_ref.1), channel_id=1, source_target_pairs={{0,16},{2,18},{4,20},{6,22},{8,24},{10,26},{12,28},{14,30},{16,0},... | collective-permute-start | bytes 221192 | tf_op jit(solution)/shard_map/ppermute | solution.py:262
  11.7 3.2 %collective-permute-start.4 = (bf16[3,64,576]{2,1,0:T(8,128)(2,1)S(1)}, bf16[3,64,576]{2,1,0:T(8,128)(2,1)S(1)}, u32[]{:S(2)}, u32[]{:S(2)}) collective-permute-start(bf16[3,64,576]{2,1,0:T(8,128)(2,1)S(1)} %get-tuple-element.28.refs_0_), channel_id=1, source_target_pairs={{0,2},{2,0},{4,6},{6,4},{8,10},{10,8},{12,14},{14,12},{16,18},{18,... | collective-permute-start | bytes 663560 | tf_op jit(solution)/shard_map/ppermute | solution.py:265
  11.8 6.6 %collective-permute-start.3 = (bf16[2,64,576]{2,1,0:T(8,128)(2,1)S(1)}, bf16[2,64,576]{2,1,0:T(8,128)(2,1)S(1)}, u32[]{:S(2)}, u32[]{:S(2)}) collective-permute-start(bf16[2,64,576]{2,1,0:T(8,128)(2,1)S(1)} %get-tuple-element.29), channel_id=1, source_target_pairs={{0,4},{2,6},{4,0},{6,2},{8,12},{10,14},{12,8},{14,10},{16,20},{18,... | collective-permute-start | bytes 442376 | tf_op jit(solution)/shard_map/ppermute | solution.py:265
  13.3 10.8 %collective-permute-start.2 = (bf16[3,64,576]{2,1,0:T(8,128)(2,1)S(1)}, bf16[3,64,576]{2,1,0:T(8,128)(2,1)S(1)}, u32[]{:S(2)}, u32[]{:S(2)}) collective-permute-start(bf16[3,64,576]{2,1,0:T(8,128)(2,1)S(1)} %get-tuple-element.28.refs_0_), channel_id=1, source_target_pairs={{0,1},{1,0},{2,3},{3,2},{4,5},{5,4},{6,7},{7,6},{8,9},{9,8},{10,11... | collective-permute-start | bytes 663560 | tf_op jit(solution)/shard_map/ppermute | solution.py:268
  18.4 8.4 %copy-start = (bf16[32,512,128]{2,1,0:T(8,128)(2,1)S(1)}, bf16[32,512,128]{2,1,0:T(8,128)(2,1)}, u32[]{:S(2)}) copy-start(bf16[32,512,128]{2,1,0:T(8,128)(2,1)} %refs_7_.1) | copy-start | bytes 12582916
  18.4 1.5 %collective-permute-start.6 = (bf16[2,64,576]{2,1,0:T(8,128)(2,1)S(1)}, bf16[2,64,576]{2,1,0:T(8,128)(2,1)S(1)}, u32[]{:S(2)}, u32[]{:S(2)}) collective-permute-start(bf16[2,64,576]{2,1,0:T(8,128)(2,1)S(1)} %collective-permute-done.3.refs_0_), channel_id=1, source_target_pairs={{0,2},{2,0},{4,6},{6,4},{8,10},{10,8},{12,14},{14,12},{16,18},{18,... | collective-permute-start | bytes 442376 | tf_op jit(solution)/shard_map/ppermute | solution.py:265
  18.4 6.6 %collective-permute-start.5 = (bf16[2,64,576]{2,1,0:T(8,128)(2,1)S(1)}, bf16[2,64,576]{2,1,0:T(8,128)(2,1)S(1)}, u32[]{:S(2)}, u32[]{:S(2)}) collective-permute-start(bf16[2,64,576]{2,1,0:T(8,128)(2,1)S(1)} %collective-permute-done.3.refs_0_), channel_id=1, source_target_pairs={{0,1},{1,0},{2,3},{3,2},{4,5},{5,4},{6,7},{7,6},{8,9},{9,8},{10,11... | collective-permute-start | bytes 442376 | tf_op jit(solution)/shard_map/ppermute | solution.py:268
  25.0 1.8 %collective-permute-start.7 = (bf16[3,64,576]{2,1,0:T(8,128)(2,1)S(1)}, bf16[3,64,576]{2,1,0:T(8,128)(2,1)S(1)}, u32[]{:S(2)}, u32[]{:S(2)}) collective-permute-start(bf16[3,64,576]{2,1,0:T(8,128)(2,1)S(1)} %collective-permute-done.2.refs_0_), channel_id=1, source_target_pairs={{0,2},{2,0},{4,6},{6,4},{8,10},{10,8},{12,14},{14,12},{16,18},{18,... | collective-permute-start | bytes 663560 | tf_op jit(solution)/shard_map/ppermute | solution.py:265
  25.0 1.7 %collective-permute-start.8 = (bf16[2,64,576]{2,1,0:T(8,128)(2,1)S(1)}, bf16[2,64,576]{2,1,0:T(8,128)(2,1)S(1)}, u32[]{:S(2)}, u32[]{:S(2)}) collective-permute-start(bf16[2,64,576]{2,1,0:T(8,128)(2,1)S(1)} %collective-permute-done.5.refs_2_), channel_id=1, source_target_pairs={{0,2},{2,0},{4,6},{6,4},{8,10},{10,8},{12,14},{14,12},{16,18},{18,... | collective-permute-start | bytes 442376 | tf_op jit(solution)/shard_map/ppermute | solution.py:265

commit v6 on v5

--- a/solution.py
+++ b/solution.py
@@ -14,7 +14,7 @@
 PLANE = 4
 GROUP = 8
 SUB = 4
-VALUE_GROUP = 8
+VALUE_GROUP = 4
 HBM = pl.BlockSpec(memory_space=pltpu.HBM)
 VMEM = pl.BlockSpec(memory_space=pltpu.VMEM)
 SMEM = pl.BlockSpec(memory_space=pltpu.SMEM)

time: 34.2 us -> 34.2 us (level)
  no operation moved by 1% of the time
where the time goes in v6:
time: 34.2 us; the launch traced here: 33.8 us
  Pallas kernels  18 us (53%)
  starting transfers between devices  10.8 us (32%)
  waiting for transfers between devices  4.7 us (14%)
    pallas_call x3, Pallas kernels, attend(): pl.pallas_call(functools.partial(attend_kernel, layout, scale, not state,...  14.4 us
    ppermute x2, starting transfers between devices, plane_shift(): lax.ppermute(array, 'ctx', [(s, (s + steps) % ctx_size) for s in range(ct...  5.67 us
    pallas_call x1, Pallas kernels, shards(): pl.pallas_call(query_kernel, out_shape=(jax.ShapeDtypeStruct((heads * row...  3.27 us
    ppermute x2, starting transfers between devices, swap_head(): return lax.ppermute(array, 'head', [(0, 1), (1, 0)])  2.98 us
    ppermute x2, waiting for transfers between devices, plane_shift(): lax.ppermute(array, 'ctx', [(s, (s + steps) % ctx_size) for s in range(ct...  2.33 us
    ppermute x5, starting transfers between devices, swap_ctx(): return lax.ppermute(array, 'ctx', [(s, s ^ bit) for s in range(ctx_size)])  2.18 us
    ppermute x5, waiting for transfers between devices, swap_ctx(): return lax.ppermute(array, 'ctx', [(s, s ^ bit) for s in range(ctx_size)])  1.49 us
    ppermute x2, waiting for transfers between devices, swap_head(): return lax.ppermute(array, 'head', [(0, 1), (1, 0)])  0.88 us
  transfers between devices with their start and end apart: 9, of which 4 were waited for; matrix products, arithmetic and copies ran while one was open for 0% of the time, Pallas kernels for 32%

profile of v6, /device:TPU:0, one launch (start us, length us, event | category | flops | bytes accessed | tf_op | source)
XLA Modules:
  0.0 33.8 jit_solution(18253447657491340624)
XLA Ops:
  0.0 0.0 copy-start.1
  0.0 0.0 copy-start.2
  0.0 0.0 copy-start.3
  0.0 3.1 %collective-permute-start = (bf16[64,576]{1,0:T(8,128)(2,1)}, bf16[64,576]{1,0:T(8,128)(2,1)S(1)}, u32[]{:S(2)}, u32[]{:S(2)}) collective-permute-start(bf16[64,576]{1,0:T(8,128)(2,1)} %own_ref.1), channel_id=1, source_target_pairs={{0,8},{2,10},{4,12},{6,14},{8,16},{10,18},{12,20},{14,22},{16,24},... | collective-permute-start | bytes 221192 | tf_op jit(solution)/shard_map/ppermute | solution.py:262
  3.1 2.6 %collective-permute-start.1 = (bf16[64,576]{1,0:T(8,128)(2,1)}, bf16[64,576]{1,0:T(8,128)(2,1)S(1)}, u32[]{:S(2)}, u32[]{:S(2)}) collective-permute-start(bf16[64,576]{1,0:T(8,128)(2,1)} %own_ref.1), channel_id=1, source_target_pairs={{0,16},{2,18},{4,20},{6,22},{8,24},{10,26},{12,28},{14,30},{16,0},... | collective-permute-start | bytes 221192 | tf_op jit(solution)/shard_map/ppermute | solution.py:262
  5.7 3.3 %queries.1 = (bf16[4096,640]{1,0:T(8,128)(2,1)S(1)}, f32[3,64,128]{2,1,0:T(8,128)S(1)}, f32[3,64,128]{2,1,0:T(8,128)S(1)}) custom-call(s32[4]{0:T(128)} %lengths_ref.5, bf16[128,4096]{1,0:T(8,128)(2,1)} %qn_hbm.1, bf16[128,2048]{1,0:T(8,128)(2,1)} %qr_hbm.1, bf16[32,128,512]{2,1,0:T(8,128)(2,1)} %ku_hbm.1), custom_call_target="tpu_custom_call" | custom-call | flops 536870912 | bytes 8388608 | tf_op jit(solution)/shard_map/queries/pallas_call | solution.py:273
  8.9 0.0 collective-permute-done.one_ref
  9.0 2.3 %collective-permute-done.1.two_ref = bf16[64,576]{1,0:T(8,128)(2,1)S(1)} collective-permute-done((bf16[64,576]{1,0:T(8,128)(2,1)}, bf16[64,576]{1,0:T(8,128)(2,1)S(1)}, u32[]{:S(2)}, u32[]{:S(2)}) %collective-permute-start.1) | collective-permute-done | bytes 73760 | tf_op jit(solution)/shard_map/ppermute | solution.py:262
  11.3 0.0 copy-done.1
  11.3 0.0 copy-done.3
  11.3 0.4 %rows.1 = (bf16[3,64,576]{2,1,0:T(8,128)(2,1)S(1)}, bf16[2,64,576]{2,1,0:T(8,128)(2,1)S(1)}) custom-call(bf16[64,576]{1,0:T(8,128)(2,1)S(1)} %copy-done.1, bf16[64,576]{1,0:T(8,128)(2,1)S(1)} %collective-permute-done.one_ref, bf16[64,576]{1,0:T(8,128)(2,1)S(1)} %collective-permute-done.1.two_ref, f32[1,512]{1,0:T(1,128)S(1)} %bitcast.1, ...), custom_call_target="tpu_custom_call" | custom-call | tf_op jit(solution)/shard_map/rows/pallas_call | solution.py:293
  11.7 0.1 collective-permute-start.4
  11.8 1.6 %collective-permute-start.3 = (bf16[2,64,576]{2,1,0:T(8,128)(2,1)S(1)}, bf16[2,64,576]{2,1,0:T(8,128)(2,1)S(1)}, u32[]{:S(2)}, u32[]{:S(2)}) collective-permute-start(bf16[2,64,576]{2,1,0:T(8,128)(2,1)S(1)} %get-tuple-element.29), channel_id=1, source_target_pairs={{0,4},{2,6},{4,0},{6,2},{8,12},{10,14},{12,8},{14,10},{16,20},{18,... | collective-permute-start | bytes 442376 | tf_op jit(solution)/shard_map/ppermute | solution.py:265
  13.3 1.5 %collective-permute-start.2 = (bf16[3,64,576]{2,1,0:T(8,128)(2,1)S(1)}, bf16[3,64,576]{2,1,0:T(8,128)(2,1)S(1)}, u32[]{:S(2)}, u32[]{:S(2)}) collective-permute-start(bf16[3,64,576]{2,1,0:T(8,128)(2,1)S(1)} %get-tuple-element.28.refs_0_), channel_id=1, source_target_pairs={{0,1},{1,0},{2,3},{3,2},{4,5},{5,4},{6,7},{7,6},{8,9},{9,8},{10,11... | collective-permute-start | bytes 663560 | tf_op jit(solution)/shard_map/ppermute | solution.py:268
  14.8 0.0 collective-permute-done.4.refs_1_
  14.8 0.0 copy-done.2
  14.8 3.3 %attend_near.1 = (f32[4096,512]{1,0:T(8,128)S(1)}, f32[4096,128]{1,0:T(8,128)S(1)}, f32[4096,128]{1,0:T(8,128)S(1)}) custom-call(s32[4]{0:T(128)S(1)} %copy-done.2, bf16[4096,640]{1,0:T(8,128)(2,1)S(1)} %get-tuple-element.25.q_ref, bf16[3,64,576]{2,1,0:T(8,128)(2,1)S(1)} %get-tuple-element.28.refs_0_, bf16[3,64,576]{2,1,0:T(8,128)(2,1)S(1)} %collective-permute-done.4.refs_1_), custom_call_target="tpu_custom_call" | custom-call | tf_op jit(solution)/shard_map/attend_near/pallas_call | solution.py:325
  18.1 0.2 collective-permute-done.3.refs_0_
  18.4 0.0 copy-start
  18.4 0.0 collective-permute-start.6
  18.4 1.5 %collective-permute-start.5 = (bf16[2,64,576]{2,1,0:T(8,128)(2,1)S(1)}, bf16[2,64,576]{2,1,0:T(8,128)(2,1)S(1)}, u32[]{:S(2)}, u32[]{:S(2)}) collective-permute-start(bf16[2,64,576]{2,1,0:T(8,128)(2,1)S(1)} %collective-permute-done.3.refs_0_), channel_id=1, source_target_pairs={{0,1},{1,0},{2,3},{3,2},{4,5},{5,4},{6,7},{7,6},{8,9},{9,8},{10,11... | collective-permute-start | bytes 442376 | tf_op jit(solution)/shard_map/ppermute | solution.py:268
  19.9 0.0 collective-permute-done.6.refs_1_
  19.9 4.2 %attend_across.1 = (f32[4096,512]{1,0:T(8,128)S(1)}, f32[4096,128]{1,0:T(8,128)S(1)}, f32[4096,128]{1,0:T(8,128)S(1)}) custom-call(s32[4]{0:T(128)S(1)} %copy-done.2, bf16[4096,640]{1,0:T(8,128)(2,1)S(1)} %get-tuple-element.25.q_ref, bf16[2,64,576]{2,1,0:T(8,128)(2,1)S(1)} %collective-permute-done.3.refs_0_, ...), custom_call_target="tpu_custom_call" | custom-call | tf_op jit(solution)/shard_map/attend_across/pallas_call | solution.py:325
  24.1 0.0 collective-permute-done.2.refs_0_
  24.1 0.9 %collective-permute-done.5.refs_2_ = bf16[2,64,576]{2,1,0:T(8,128)(2,1)S(1)} collective-permute-done((bf16[2,64,576]{2,1,0:T(8,128)(2,1)S(1)}, bf16[2,64,576]{2,1,0:T(8,128)(2,1)S(1)}, u32[]{:S(2)}, u32[]{:S(2)}) %collective-permute-start.5) | collective-permute-done | bytes 147488 | tf_op jit(solution)/shard_map/ppermute | solution.py:268
  25.0 0.0 collective-permute-start.7
  25.0 0.5 %collective-permute-start.8 = (bf16[2,64,576]{2,1,0:T(8,128)(2,1)S(1)}, bf16[2,64,576]{2,1,0:T(8,128)(2,1)S(1)}, u32[]{:S(2)}, u32[]{:S(2)}) collective-permute-start(bf16[2,64,576]{2,1,0:T(8,128)(2,1)S(1)} %collective-permute-done.5.refs_2_), channel_id=1, source_target_pairs={{0,2},{2,0},{4,6},{6,4},{8,10},{10,8},{12,14},{14,12},{16,18},{18,... | collective-permute-start | bytes 442376 | tf_op jit(solution)/shard_map/ppermute | solution.py:265
  25.5 1.2 %collective-permute-done.8.refs_3_ = bf16[2,64,576]{2,1,0:T(8,128)(2,1)S(1)} collective-permute-done((bf16[2,64,576]{2,1,0:T(8,128)(2,1)S(1)}, bf16[2,64,576]{2,1,0:T(8,128)(2,1)S(1)}, u32[]{:S(2)}, u32[]{:S(2)}) %collective-permute-start.8) | collective-permute-done | bytes 147488 | tf_op jit(solution)/shard_map/ppermute | solution.py:265
  26.7 0.0 collective-permute-done.7.refs_1_
  26.7 0.0 copy-done
  26.7 6.9 %attend_far.1 = bf16[128,4096]{1,0:T(8,128)(2,1)} custom-call(s32[4]{0:T(128)S(1)} %copy-done.2, bf16[4096,640]{1,0:T(8,128)(2,1)S(1)} %get-tuple-element.25.q_ref, bf16[3,64,576]{2,1,0:T(8,128)(2,1)S(1)} %collective-permute-done.2.refs_0_, bf16[3,64,576]{2,1,0:T(8,128)(2,1)S(1)} %collective-permute-done.7.refs_1_, ...), custom_call_target="tpu_custom_call" | custom-call | tf_op jit(solution)/shard_map/attend_far/pallas_call | solution.py:325
Async XLA Ops:
  0.0 11.3 %copy-start.1 = (bf16[64,576]{1,0:T(8,128)(2,1)S(1)}, bf16[64,576]{1,0:T(8,128)(2,1)}, u32[]{:S(2)}) copy-start(bf16[64,576]{1,0:T(8,128)(2,1)} %own_ref.1) | copy-start | bytes 221188
  0.0 14.8 %copy-start.2 = (s32[4]{0:T(128)S(1)}, s32[4]{0:T(128)}, u32[]{:S(2)}) copy-start(s32[4]{0:T(128)} %lengths_ref.5) | copy-start | bytes 52
  0.0 11.3 %copy-start.3 = (f32[512]{0:T(512)S(1)}, f32[512]{0:T(512)}, u32[]{:S(2)}) copy-start(f32[512]{0:T(512)} %param.8) | copy-start | bytes 6148
  0.0 8.9 %collective-permute-start = (bf16[64,576]{1,0:T(8,128)(2,1)}, bf16[64,576]{1,0:T(8,128)(2,1)S(1)}, u32[]{:S(2)}, u32[]{:S(2)}) collective-permute-start(bf16[64,576]{1,0:T(8,128)(2,1)} %own_ref.1), channel_id=1, source_target_pairs={{0,8},{2,10},{4,12},{6,14},{8,16},{10,18},{12,20},{14,22},{16,24},... | collective-permute-start | bytes 221192 | tf_op jit(solution)/shard_map/ppermute | solution.py:262
  3.1 8.2 %collective-permute-start.1 = (bf16[64,576]{1,0:T(8,128)(2,1)}, bf16[64,576]{1,0:T(8,128)(2,1)S(1)}, u32[]{:S(2)}, u32[]{:S(2)}) collective-permute-start(bf16[64,576]{1,0:T(8,128)(2,1)} %own_ref.1), channel_id=1, source_target_pairs={{0,16},{2,18},{4,20},{6,22},{8,24},{10,26},{12,28},{14,30},{16,0},... | collective-permute-start | bytes 221192 | tf_op jit(solution)/shard_map/ppermute | solution.py:262
  11.7 3.2 %collective-permute-start.4 = (bf16[3,64,576]{2,1,0:T(8,128)(2,1)S(1)}, bf16[3,64,576]{2,1,0:T(8,128)(2,1)S(1)}, u32[]{:S(2)}, u32[]{:S(2)}) collective-permute-start(bf16[3,64,576]{2,1,0:T(8,128)(2,1)S(1)} %get-tuple-element.28.refs_0_), channel_id=1, source_target_pairs={{0,2},{2,0},{4,6},{6,4},{8,10},{10,8},{12,14},{14,12},{16,18},{18,... | collective-permute-start | bytes 663560 | tf_op jit(solution)/shard_map/ppermute | solution.py:265
  11.8 6.6 %collective-permute-start.3 = (bf16[2,64,576]{2,1,0:T(8,128)(2,1)S(1)}, bf16[2,64,576]{2,1,0:T(8,128)(2,1)S(1)}, u32[]{:S(2)}, u32[]{:S(2)}) collective-permute-start(bf16[2,64,576]{2,1,0:T(8,128)(2,1)S(1)} %get-tuple-element.29), channel_id=1, source_target_pairs={{0,4},{2,6},{4,0},{6,2},{8,12},{10,14},{12,8},{14,10},{16,20},{18,... | collective-permute-start | bytes 442376 | tf_op jit(solution)/shard_map/ppermute | solution.py:265
  13.3 10.8 %collective-permute-start.2 = (bf16[3,64,576]{2,1,0:T(8,128)(2,1)S(1)}, bf16[3,64,576]{2,1,0:T(8,128)(2,1)S(1)}, u32[]{:S(2)}, u32[]{:S(2)}) collective-permute-start(bf16[3,64,576]{2,1,0:T(8,128)(2,1)S(1)} %get-tuple-element.28.refs_0_), channel_id=1, source_target_pairs={{0,1},{1,0},{2,3},{3,2},{4,5},{5,4},{6,7},{7,6},{8,9},{9,8},{10,11... | collective-permute-start | bytes 663560 | tf_op jit(solution)/shard_map/ppermute | solution.py:268
  18.4 8.4 %copy-start = (bf16[32,512,128]{2,1,0:T(8,128)(2,1)S(1)}, bf16[32,512,128]{2,1,0:T(8,128)(2,1)}, u32[]{:S(2)}) copy-start(bf16[32,512,128]{2,1,0:T(8,128)(2,1)} %refs_7_.1) | copy-start | bytes 12582916
  18.4 1.5 %collective-permute-start.6 = (bf16[2,64,576]{2,1,0:T(8,128)(2,1)S(1)}, bf16[2,64,576]{2,1,0:T(8,128)(2,1)S(1)}, u32[]{:S(2)}, u32[]{:S(2)}) collective-permute-start(bf16[2,64,576]{2,1,0:T(8,128)(2,1)S(1)} %collective-permute-done.3.refs_0_), channel_id=1, source_target_pairs={{0,2},{2,0},{4,6},{6,4},{8,10},{10,8},{12,14},{14,12},{16,18},{18,... | collective-permute-start | bytes 442376 | tf_op jit(solution)/shard_map/ppermute | solution.py:265
  18.4 6.6 %collective-permute-start.5 = (bf16[2,64,576]{2,1,0:T(8,128)(2,1)S(1)}, bf16[2,64,576]{2,1,0:T(8,128)(2,1)S(1)}, u32[]{:S(2)}, u32[]{:S(2)}) collective-permute-start(bf16[2,64,576]{2,1,0:T(8,128)(2,1)S(1)} %collective-permute-done.3.refs_0_), channel_id=1, source_target_pairs={{0,1},{1,0},{2,3},{3,2},{4,5},{5,4},{6,7},{7,6},{8,9},{9,8},{10,11... | collective-permute-start | bytes 442376 | tf_op jit(solution)/shard_map/ppermute | solution.py:268
  25.0 1.8 %collective-permute-start.7 = (bf16[3,64,576]{2,1,0:T(8,128)(2,1)S(1)}, bf16[3,64,576]{2,1,0:T(8,128)(2,1)S(1)}, u32[]{:S(2)}, u32[]{:S(2)}) collective-permute-start(bf16[3,64,576]{2,1,0:T(8,128)(2,1)S(1)} %collective-permute-done.2.refs_0_), channel_id=1, source_target_pairs={{0,2},{2,0},{4,6},{6,4},{8,10},{10,8},{12,14},{14,12},{16,18},{18,... | collective-permute-start | bytes 663560 | tf_op jit(solution)/shard_map/ppermute | solution.py:265
  25.0 1.7 %collective-permute-start.8 = (bf16[2,64,576]{2,1,0:T(8,128)(2,1)S(1)}, bf16[2,64,576]{2,1,0:T(8,128)(2,1)S(1)}, u32[]{:S(2)}, u32[]{:S(2)}) collective-permute-start(bf16[2,64,576]{2,1,0:T(8,128)(2,1)S(1)} %collective-permute-done.5.refs_2_), channel_id=1, source_target_pairs={{0,2},{2,0},{4,6},{6,4},{8,10},{10,8},{12,14},{14,12},{16,18},{18,... | collective-permute-start | bytes 442376 | tf_op jit(solution)/shard_map/ppermute | solution.py:265
